TPU v7x, 32 devices: a whole 2x2x4 slice. The times are simulated.
32 devices in a mesh: group: 2 (over x), rows: 16 (over z, y, core).
Axes of the slice: x: 2, y: 2, z: 4, core: 2. Of those that a mesh axis runs over, the one named last changes fastest.
Arguments:
- spectra: float32 [4, 1024, 6144], P('group', 'rows'), parts along dimension 0, may hold values from -6 to 6
- plane: float32 [1024, 6144], P('rows'), may hold values from -6 to 6
- interval_edges: int32 [12, 2], replicated, may hold values from 0 to 128
- tile_shifts: int32 [4, 12, 2], P('group'), parts along dimension 0, may hold values from -8 to 8, as said below
Outputs:
- correlation: float32 [4, 1024, 6144], P('group', 'rows'), parts along dimension 0
- aligned_spectra: float32 [4, 1024, 6144], P('group', 'rows'), parts along dimension 0
There are 2 independent parts, one for each index of `group`. A program takes and returns all parts, laid end to end along the dimension named above; an argument that names none is the same for every part. Nothing has to cross between parts.
Inputs may be any that keep to these rules, and one draw needn't show every extreme that they name: `tile_shifts`: both shifts lie in -8 to 8; the 1024 shift equals 8 for some tile and -8 for another in every draw.
All inputs are finite; a program needn't handle non-finite values.
Results may differ from a plain program's by a relative error of at most 0.000098.
Values sent between devices are 32-bit elements; how exact they have to be, the bound alone decides.
A program may use at most 128 MiB of HBM per device.

v0:
```python
import math

import jax
import jax.numpy as jnp
import numpy as np
from jax import lax
from jax.experimental import pallas as pl
from jax.experimental.pallas import tpu as pltpu
from jax.sharding import PartitionSpec as P

F1 = 1024
TF2 = 512
HALF = TF2 // 2
MAXS = 8
LANES = 128

exact = lax.Precision.HIGH
full = lax.Precision.HIGHEST


def trig(rows, columns, modulus):
    angle = np.outer(np.arange(rows), np.arange(columns)) % modulus * (2.0 * math.pi / modulus)
    return np.cos(angle), np.sin(angle)


def column_table():
    return np.stack(trig(F1, F1, F1))


def row_tables(span):
    groups = HALF // span
    cosine, sine = trig(TF2, HALF, TF2)
    alternate = np.where(np.arange(TF2) % 2 == 0, 1.0, -1.0)
    forward_imag = -sine
    forward_imag[:, 0] = alternate
    forward = np.stack([cosine, forward_imag], axis=1)
    forward = forward.reshape(TF2, 2, groups, span).transpose(0, 2, 1, 3)
    forward = forward.reshape(TF2, groups, 2 * span)
    weights = np.where(np.arange(HALF) == 0, 1.0, 2.0)[None, :]
    inverse_imag = -2.0 * sine
    inverse_imag[:, 0] = alternate
    inverse = np.stack([weights * cosine, inverse_imag], axis=1)
    inverse = inverse.reshape(TF2, 2, groups, span).transpose(2, 1, 3, 0)
    inverse = inverse.reshape(groups, 2 * span, TF2) * float(F1 * TF2) ** (-1.5)
    return forward, inverse


def align_kernel(shifts, body, above, below, out, padded):
    spectrum = pl.program_id(0)
    height, breadth = body.shape[1:]
    total = height + 2 * MAXS
    margin = jnp.zeros((total, LANES), jnp.float32)
    padded[:, :LANES] = margin
    padded[:, LANES + breadth :] = margin
    padded[:MAXS, LANES : LANES + breadth] = above[0]
    padded[MAXS : MAXS + height, LANES : LANES + breadth] = body[0]
    padded[MAXS + height :, LANES : LANES + breadth] = below[0]
    window = TF2 + 2 * LANES
    for tile in range(breadth // TF2):
        down = shifts[spectrum, tile, 0]
        right = shifts[spectrum, tile, 1]
        part = padded[:, tile * TF2 : tile * TF2 + window]
        part = pltpu.roll(part, lax.rem(right + window, window), 1)[:, LANES : LANES + TF2]
        part = pltpu.roll(part, lax.rem(down + total, total), 0)
        out[0, :, tile * TF2 : (tile + 1) * TF2] = part[MAXS : MAXS + height]


def aligned(spectra, tile_shifts):
    number, height, breadth = spectra.shape
    count = lax.axis_size("rows")
    head = spectra[:, :MAXS]
    tail = spectra[:, height - MAXS :]
    above = lax.ppermute(tail, "rows", [(i, i + 1) for i in range(count - 1)])
    below = lax.ppermute(head, "rows", [(i + 1, i) for i in range(count - 1)])
    whole = pl.BlockSpec((1, height, breadth), lambda s: (s, 0, 0))
    edge = pl.BlockSpec((1, MAXS, breadth), lambda s: (s, 0, 0))
    return pl.pallas_call(
        align_kernel,
        grid=(number,),
        out_shape=jax.ShapeDtypeStruct(spectra.shape, jnp.float32),
        in_specs=[pl.BlockSpec(memory_space=pltpu.SMEM), whole, edge, edge],
        out_specs=whole,
        scratch_shapes=[pltpu.VMEM((height + 2 * MAXS, breadth + 2 * LANES), jnp.float32)],
        compiler_params=pltpu.CompilerParams(vmem_limit_bytes=24 * 2**20),
        cost_estimate=pl.CostEstimate(
            flops=20 * spectra.size, bytes_accessed=8 * spectra.size, transcendentals=0
        ),
    )(tile_shifts, spectra, above, below)


def plain_products(plane_columns, received, packed):
    count, local, height, width = plane_columns.shape
    span = width // 2
    columns = column_table().astype(np.float32)

    def halves(block):
        pencil = block.transpose(0, 2, 1, 3).reshape(F1, local * width)
        both = jnp.einsum("pkn,nl->pkl", columns, pencil, precision=exact)
        return both.reshape(2, F1, local, 2, span)

    def spectrum_of(both):
        cosine, sine = both[0], both[1]
        return cosine[:, :, 0] + sine[:, :, 1], cosine[:, :, 1] - sine[:, :, 0]

    plane_halves = halves(plane_columns)
    plane_real, plane_imag = spectrum_of(plane_halves)

    def back(block):
        both = halves(block)
        real, imag = spectrum_of(both)
        out_real = real * plane_real + imag * plane_imag
        out_imag = imag * plane_real - real * plane_imag
        cosine, sine = both[0], both[1]
        pc, ps = plane_halves[0], plane_halves[1]
        mask = packed[None, :, None, :]
        first = jnp.stack([out_real, out_imag], axis=2)
        second = jnp.stack([-out_imag, out_real], axis=2)
        first = jnp.where(mask, cosine * pc + sine * ps, first)
        second = jnp.where(mask, sine * pc - cosine * ps, second)
        pair = jnp.stack([first, second]).reshape(2, F1, local * width)
        rows = jnp.einsum("pkn,pnl->kl", columns, pair, precision=exact)
        return rows.reshape(count, height, local, width).transpose(0, 2, 1, 3)

    return [back(block) for block in received]


def split(values):
    high = values.astype(jnp.bfloat16)
    return high, (values - high.astype(jnp.float32)).astype(jnp.bfloat16)


def product_3(table_high, table_low, rows, high, low):
    def dot(a, b):
        return jnp.dot(a, b, preferred_element_type=jnp.float32)

    top = table_high[rows, :]
    return dot(top, high) + (dot(top, low) + dot(table_low[rows, :], high))


CHUNK = 256


def forward_halves(table_high, table_low, block, both, high, low):
    count, local, height, width = block.shape
    for source in range(count):
        for part in range(local):
            rows = slice(source * height, (source + 1) * height)
            lanes = slice(part * width, (part + 1) * width)
            high[rows, lanes], low[rows, lanes] = split(block[source, part])

    @pl.loop(0, 2 * F1 // CHUNK)
    def _(step):
        rows = pl.ds(pl.multiple_of(step * CHUNK, CHUNK), CHUNK)
        both[rows, :] = product_3(table_high, table_low, rows, high[...], low[...])


def product_kernel(
    table_high, table_low, block, plane_both, packed, out, both, high, low, pair_high, pair_low
):
    count, local, height, width = block.shape
    forward_halves(table_high, table_low, block, both, high, low)
    rows_per = 64
    lane = lax.broadcasted_iota(jnp.int32, (rows_per, width), 1)
    is_real = lane < width // 2
    sign = jnp.where(is_real, 1.0, -1.0).astype(jnp.float32)

    def swap(values):
        return pltpu.roll(values, width // 2, 1)

    @pl.loop(0, F1 // rows_per)
    def _(step):
        top = pl.ds(pl.multiple_of(step * rows_per, rows_per), rows_per)
        bottom = pl.ds(pl.multiple_of(F1 + step * rows_per, rows_per), rows_per)
        for part in range(local):
            lanes = slice(part * width, (part + 1) * width)
            c, s = both[top, lanes], both[bottom, lanes]
            pc, ps = plane_both[top, lanes], plane_both[bottom, lanes]
            value = c + sign * swap(s)
            plane_value = pc + sign * swap(ps)
            same = value * plane_value
            cross = swap(value) * plane_value
            product = jnp.where(is_real, same + swap(same), swap(cross) - cross)
            alone = packed[0:1, lanes] > 0.5
            first = jnp.where(alone, c * pc + s * ps, product)
            second = jnp.where(alone, s * pc - c * ps, -sign * swap(product))
            pair_high[top, lanes], pair_low[top, lanes] = split(first)
            pair_high[bottom, lanes], pair_low[bottom, lanes] = split(second)

    per_step = CHUNK // height

    @pl.loop(0, F1 // CHUNK)
    def _(step):
        total = jnp.zeros((CHUNK, local * width), jnp.float32)
        for side in range(2):
            rows = pl.ds(pl.multiple_of(side * F1 + step * CHUNK, CHUNK), CHUNK)
            own = slice(side * F1, (side + 1) * F1)
            total += product_3(table_high, table_low, rows, pair_high[own], pair_low[own])
        for place in range(per_step):
            for part in range(local):
                out[step * per_step + place, part] = total[
                    place * height : (place + 1) * height, part * width : (part + 1) * width
                ]


def column_parts():
    return split_table(column_table().reshape(2 * F1, F1))


def kernel_plane(plane_columns):
    breadth = plane_columns.shape[1] * plane_columns.shape[3]
    space = pl.BlockSpec(memory_space=pltpu.VMEM)
    return pl.pallas_call(
        forward_halves,
        out_shape=jax.ShapeDtypeStruct((2 * F1, breadth), jnp.float32),
        in_specs=[space] * 3,
        out_specs=space,
        scratch_shapes=[pltpu.VMEM((F1, breadth), jnp.bfloat16)] * 2,
        compiler_params=pltpu.CompilerParams(vmem_limit_bytes=44 * 2**20),
        cost_estimate=pl.CostEstimate(
            flops=12 * F1 * F1 * breadth, bytes_accessed=8 * F1 * F1, transcendentals=0
        ),
    )(*column_parts(), plane_columns)


def kernel_products(plane_both, received, packed):
    breadth = plane_both.shape[1]
    lanes = jnp.stack([packed, packed], axis=1).reshape(1, breadth).astype(jnp.float32)
    space = pl.BlockSpec(memory_space=pltpu.VMEM)
    halves_shape = (2 * F1, breadth)
    call = pl.pallas_call(
        product_kernel,
        out_shape=jax.ShapeDtypeStruct(received[0].shape, jnp.float32),
        in_specs=[space] * 5,
        out_specs=space,
        scratch_shapes=[pltpu.VMEM(halves_shape, jnp.float32)]
        + [pltpu.VMEM((F1, breadth), jnp.bfloat16)] * 2
        + [pltpu.VMEM(halves_shape, jnp.bfloat16)] * 2,
        compiler_params=pltpu.CompilerParams(vmem_limit_bytes=44 * 2**20),
        cost_estimate=pl.CostEstimate(
            flops=24 * F1 * F1 * breadth, bytes_accessed=8 * F1 * F1, transcendentals=0
        ),
    )
    return [call(*column_parts(), block, plane_both, lanes) for block in received]


def product_of(values, table_high, table_low):
    high, low = split(values)

    def dot(a, b):
        return jnp.dot(a, b, preferred_element_type=jnp.float32)

    count = values.shape[0]
    both = dot(jnp.concatenate([high, low], axis=0), table_high)
    return both[:count] + (both[count:] + dot(high, table_low))


def bins_kernel(keeper, rows, table_high, table_low, out):
    height, breadth = rows.shape
    groups = TF2 // LANES
    values = rows[...] * keeper[...]
    tiles = [values[:, start : start + TF2] for start in range(0, breadth, TF2)]
    bins = product_of(jnp.concatenate(tiles, axis=0), table_high[...], table_low[...])
    for tile in range(len(tiles)):
        for group in range(groups):
            out[tile * groups + group] = bins[
                tile * height : (tile + 1) * height, group * LANES : (group + 1) * LANES
            ]


def rows_kernel(*refs):
    blocks, (table_high, table_low, out) = refs[:-3], refs[-3:]
    granules, height = blocks[0].shape[:2]
    groups = TF2 // LANES
    places = [(s, t) for s in range(len(blocks)) for t in range(granules // groups)]
    parts = [
        jnp.concatenate([blocks[s][t * groups + group] for group in range(groups)], axis=1)
        for s, t in places
    ]
    rows = product_of(jnp.concatenate(parts, axis=0), table_high[...], table_low[...])
    for place, (s, t) in enumerate(places):
        out[s, :, t * TF2 : (t + 1) * TF2] = rows[place * height : (place + 1) * height]


def tiles_at_once(tiles):
    return 3 if tiles % 3 == 0 else 2 if tiles % 2 == 0 else 1


def split_table(table):
    high = table.astype(jnp.bfloat16)
    return high, (table - high.astype(np.float64)).astype(jnp.bfloat16)


def kernel_bins(spectra, index, keeper, table):
    height, breadth = spectra.shape[1:]
    tiles, groups = breadth // TF2, TF2 // LANES
    step = tiles_at_once(tiles)
    fixed = pl.BlockSpec((TF2, TF2), lambda b: (0, 0))
    return pl.pallas_call(
        bins_kernel,
        grid=(tiles // step,),
        out_shape=jax.ShapeDtypeStruct((tiles * groups, height, LANES), jnp.float32),
        in_specs=[
            pl.BlockSpec((1, step * TF2), lambda b: (0, b)),
            pl.BlockSpec((None, height, step * TF2), lambda b: (index, 0, b)),
            fixed,
            fixed,
        ],
        out_specs=pl.BlockSpec((step * groups, height, LANES), lambda b: (b, 0, 0)),
        compiler_params=pltpu.CompilerParams(vmem_limit_bytes=24 * 2**20),
        cost_estimate=pl.CostEstimate(
            flops=6 * height * breadth * TF2, bytes_accessed=8 * height * breadth, transcendentals=0
        ),
    )(keeper, spectra, *split_table(table))


def kernel_rows(blocks, table):
    granules, height = blocks[0].shape[:2]
    groups = TF2 // LANES
    tiles = granules // groups
    number = len(blocks)
    step = tiles_at_once(tiles)
    fixed = pl.BlockSpec((TF2, TF2), lambda b: (0, 0))
    return pl.pallas_call(
        rows_kernel,
        grid=(tiles // step,),
        out_shape=jax.ShapeDtypeStruct((number, height, tiles * TF2), jnp.float32),
        in_specs=[pl.BlockSpec((step * groups, height, LANES), lambda b: (b, 0, 0))] * number
        + [fixed, fixed],
        out_specs=pl.BlockSpec((number, height, step * TF2), lambda b: (0, 0, b)),
        compiler_params=pltpu.CompilerParams(vmem_limit_bytes=24 * 2**20),
    )(*blocks, *split_table(table))


def per_device(spectra, plane, interval_edges, tile_shifts):
    number, height, breadth = spectra.shape
    count = lax.axis_size("rows")
    tiles = breadth // TF2
    span = math.gcd(breadth // 2 // count, HALF)
    groups = HALF // span
    width = 2 * span
    local = tiles * groups // count
    forward, inverse = row_tables(span)

    point = jnp.arange(TF2, dtype=jnp.int32)[None, :]
    inside = (point >= interval_edges[:, 0:1]) & (point < TF2 - interval_edges[:, 1:2])
    keeper = jnp.where(inside, 1.0, 0.0).astype(jnp.float32).reshape(1, breadth)

    cohorts = lax.axis_size("group")
    share = height // cohorts
    whole_tiles = width == LANES and share % 16 == 0

    def to_columns(rows, index, kept, after=None):
        held = rows.shape[1]
        if whole_tiles:
            bins = kernel_bins(rows, index, kept, forward.reshape(TF2, TF2))
        else:
            blocks = (rows[index] * kept).reshape(held, tiles, TF2)
            table = forward.astype(np.float32)
            bins = jnp.einsum("rbn,njl->bjrl", blocks, table, precision=full)
        sent = bins.reshape(count, local, held, width)
        if after is not None:
            sent, _ = lax.optimization_barrier((sent, after))
        return lax.all_to_all(sent, "rows", split_axis=0, concat_axis=0, tiled=True)

    granule = lax.axis_index("rows") * local + jnp.arange(local, dtype=jnp.int32)
    packed = (granule % groups == 0)[:, None] & (jnp.arange(span) == 0)[None, :]
    own = lax.axis_index("group")
    plane_rows = lax.dynamic_slice_in_dim(plane, own * share, share, axis=0)
    mine = to_columns(plane_rows[None], 0, jnp.ones_like(keeper))
    if cohorts == 2:
        other = lax.ppermute(mine, "group", [(0, 1), (1, 0)])
        ordered = [jnp.where(own == 0, mine, other), jnp.where(own == 0, other, mine)]
        plane_columns = jnp.concatenate(ordered, axis=2)
    else:
        plane_columns = lax.all_gather(mine, "group", axis=2, tiled=True)
    plane_both = kernel_plane(plane_columns) if whole_tiles else None
    received = [to_columns(spectra, s, keeper, plane_both if s else None) for s in range(number)]
    aligned_spectra = aligned(spectra, tile_shifts)
    if whole_tiles:
        products = kernel_products(plane_both, received, packed)
    else:
        products = plain_products(plane_columns, received, packed)
    returned = [
        lax.all_to_all(block, "rows", split_axis=0, concat_axis=0, tiled=True)
        for block in products
    ]

    if whole_tiles:
        blocks = [block.reshape(tiles * groups, height, width) for block in returned]
        return (kernel_rows(blocks, inverse.reshape(TF2, TF2)), aligned_spectra)

    def to_rows(block):
        bins = block.reshape(tiles, groups, height, width)
        table = inverse.astype(np.float32)
        return jnp.einsum("bjrl,jln->rbn", bins, table, precision=full).reshape(height, breadth)

    correlation = jnp.stack([to_rows(block) for block in returned])
    return (correlation, aligned_spectra)


def solution(mesh):
    placed = (P("group", "rows", None), P("rows", None), P(), P("group", None, None))
    return jax.shard_map(
        per_device,
        mesh=mesh,
        in_specs=placed,
        out_specs=(P("group", "rows", None), P("group", "rows", None)),
        check_vma=False,
    )
```

profile of v0, /device:TPU:15, one launch (start us, length us, event | category | flops | bytes accessed | tf_op | source)
XLA Modules:
  0.0 214.1 jit_solution(595569011436196446)
XLA Ops:
  2.3 2.5 %shard_map.186 = f32[48,32,128]{2,1,0:T(8,128)} custom-call(f32[1,6144]{1,0:T(1,128)S(1)} %broadcast_in_dim.19.keeper, f32[1,32,6144]{2,1,0:T(8,128)S(1)} %dynamic-slice_bitcast_fusion.rows, bf16[512,512]{1,0:T(8,128)(2,1)S(1)} %copy-done.4, bf16[512,512]{1,0:T(8,128)(2,1)S(1)} %copy-done.5), custom_call_target="tpu_custom_call" | custom-call | flops 603979776 | bytes 1572864 | tf_op jit(solution)/shard_map/pallas_call | solution.py:298
  4.8 6.6 %all-to-all-start.1 = ((f32[16,3,32,128]{3,2,1,0:T(8,128)}), f32[16,3,32,128]{3,2,1,0:T(8,128)S(1)}, u32[]{:S(2)}, u32[]{:S(2)}) async-start(f32[16,3,32,128]{3,2,1,0:T(8,128)} %bitcast.4), calls=%async_computation.1 | async-start | bytes 1572864 | tf_op jit(solution)/shard_map/all_to_all | solution.py:363
  13.3 3.0 %shard_map.185 = f32[48,64,128]{2,1,0:T(8,128)} custom-call(f32[1,6144]{1,0:T(1,128)S(1)} %bitcast.16, f32[2,64,6144]{2,1,0:T(8,128)S(1)} %copy-done.1, bf16[512,512]{1,0:T(8,128)(2,1)S(1)} %copy-done.4, bf16[512,512]{1,0:T(8,128)(2,1)S(1)} %copy-done.5), custom_call_target="tpu_custom_call" | custom-call | flops 1207959552 | bytes 3145728 | tf_op jit(solution)/shard_map/pallas_call | solution.py:298
  16.3 14.2 %all-to-all-done.1 = f32[16,3,32,128]{3,2,1,0:T(8,128)S(1)} async-done(((f32[16,3,32,128]{3,2,1,0:T(8,128)}), f32[16,3,32,128]{3,2,1,0:T(8,128)S(1)}, u32[]{:S(2)}, u32[]{:S(2)}) %all-to-all-start.1) | async-done | bytes 786464 | tf_op jit(solution)/shard_map/all_to_all | solution.py:363
  30.6 5.0 %all-to-all-start = ((f32[16,3,64,128]{3,2,1,0:T(8,128)}), f32[16,3,64,128]{3,2,1,0:T(8,128)}, u32[]{:S(2)}, u32[]{:S(2)}) async-start(f32[16,3,64,128]{3,2,1,0:T(8,128)} %bitcast.2), calls=%async_computation | async-start | bytes 3145728 | tf_op jit(solution)/shard_map/all_to_all | solution.py:363
  37.6 3.0 %shard_map.189 = f32[48,64,128]{2,1,0:T(8,128)} custom-call(f32[1,6144]{1,0:T(1,128)S(1)} %bitcast.17, f32[2,64,6144]{2,1,0:T(8,128)S(1)} %copy-done.2, bf16[512,512]{1,0:T(8,128)(2,1)S(1)} %copy-done.4, bf16[512,512]{1,0:T(8,128)(2,1)S(1)} %copy-done.5), custom_call_target="tpu_custom_call" | custom-call | flops 1207959552 | bytes 3145728 | tf_op jit(solution)/shard_map/pallas_call | solution.py:298
  40.7 13.7 %collective-permute-done = f32[16,3,32,128]{3,2,1,0:T(8,128)} collective-permute-done((f32[16,3,32,128]{3,2,1,0:T(8,128)S(1)}, f32[16,3,32,128]{3,2,1,0:T(8,128)}, u32[]{:S(2)}, u32[]{:S(2)}) %collective-permute-start) | collective-permute-done | bytes 786464 | tf_op jit(solution)/shard_map/ppermute | solution.py:371
  56.8 10.3 %shard_map.187.plane_both = f32[2048,384]{1,0:T(8,128)S(1)} custom-call(bf16[2048,1024]{1,0:T(8,128)(2,1)S(1)} %copy-done.12, bf16[2048,1024]{1,0:T(8,128)(2,1)} %constant.54.clone.table_low, f32[16,3,64,128]{3,2,1,0:T(8,128)S(1)} %pad_maximum_fusion.block), custom_call_target="tpu_custom_call" | custom-call | flops 4831838208 | bytes 8388608 | tf_op jit(solution)/shard_map/pallas_call | solution.py:212
  68.8 3.0 %all-to-all-done.block = f32[16,3,64,128]{3,2,1,0:T(8,128)} async-done(((f32[16,3,64,128]{3,2,1,0:T(8,128)}), f32[16,3,64,128]{3,2,1,0:T(8,128)}, u32[]{:S(2)}, u32[]{:S(2)}) %all-to-all-start) | async-done | bytes 1572896 | tf_op jit(solution)/shard_map/all_to_all | solution.py:363
  71.8 4.9 %all-to-all-start.3 = ((f32[16,3,64,128]{3,2,1,0:T(8,128)}), f32[16,3,64,128]{3,2,1,0:T(8,128)S(1)}, u32[]{:S(2)}, u32[]{:S(2)}) async-start(f32[16,3,64,128]{3,2,1,0:T(8,128)} %bitcast.6), calls=%async_computation.3 | async-start | bytes 3145728 | tf_op jit(solution)/shard_map/all_to_all | solution.py:363
  76.9 1.9 copy-done.14
  78.8 24.2 %shard_map.188 = f32[16,3,64,128]{3,2,1,0:T(8,128)S(1)} custom-call(bf16[2048,1024]{1,0:T(8,128)(2,1)} %constant.53.clone.table_high, bf16[2048,1024]{1,0:T(8,128)(2,1)} %constant.54.clone.table_low, f32[16,3,64,128]{3,2,1,0:T(8,128)} %all-to-all-done.block, f32[2048,384]{1,0:T(8,128)S(1)} %copy-done.14, f32[1,384]{1,0:T(1,128)S(1)} %reshape.153.packed), custom_call_target="tpu_custom_call" | custom-call | flops 9663676416 | bytes 8388608 | tf_op jit(solution)/shard_map/pallas_call | solution.py:243
  104.1 8.7 %all-to-all-done.3.block = f32[16,3,64,128]{3,2,1,0:T(8,128)S(1)} async-done(((f32[16,3,64,128]{3,2,1,0:T(8,128)}), f32[16,3,64,128]{3,2,1,0:T(8,128)S(1)}, u32[]{:S(2)}, u32[]{:S(2)}) %all-to-all-start.3) | async-done | bytes 1572896 | tf_op jit(solution)/shard_map/all_to_all | solution.py:363
  114.1 4.9 %all-to-all-start.2 = ((f32[16,3,64,128]{3,2,1,0:T(8,128)}), f32[16,3,64,128]{3,2,1,0:T(8,128)S(1)}, u32[]{:S(2)}, u32[]{:S(2)}) async-start(f32[16,3,64,128]{3,2,1,0:T(8,128)} %copy-done.9), calls=%async_computation.2 | async-start | bytes 3145728 | tf_op jit(solution)/shard_map/all_to_all | solution.py:384
  122.3 23.8 %shard_map.190 = f32[16,3,64,128]{3,2,1,0:T(8,128)S(1)} custom-call(bf16[2048,1024]{1,0:T(8,128)(2,1)} %constant.53.clone.table_high, bf16[2048,1024]{1,0:T(8,128)(2,1)} %constant.54.clone.table_low, f32[16,3,64,128]{3,2,1,0:T(8,128)S(1)} %copy-done.8, f32[2048,384]{1,0:T(8,128)S(1)} %copy-done.15, f32[1,384]{1,0:T(1,128)S(1)} %reshape.153.packed), custom_call_target="tpu_custom_call" | custom-call | flops 9663676416 | bytes 8388608 | tf_op jit(solution)/shard_map/pallas_call | solution.py:243
  147.2 7.9 %all-to-all-done.2 = f32[16,3,64,128]{3,2,1,0:T(8,128)S(1)} async-done(((f32[16,3,64,128]{3,2,1,0:T(8,128)}), f32[16,3,64,128]{3,2,1,0:T(8,128)S(1)}, u32[]{:S(2)}, u32[]{:S(2)}) %all-to-all-start.2) | async-done | bytes 1572896 | tf_op jit(solution)/shard_map/all_to_all | solution.py:384
  155.2 4.9 %all-to-all-start.4 = ((f32[16,3,64,128]{3,2,1,0:T(8,128)}), f32[16,3,64,128]{3,2,1,0:T(8,128)}, u32[]{:S(2)}, u32[]{:S(2)}) async-start(f32[16,3,64,128]{3,2,1,0:T(8,128)} %copy-done.6), calls=%async_computation.4 | async-start | bytes 3145728 | tf_op jit(solution)/shard_map/all_to_all | solution.py:384
  160.1 2.0 fusion.3
  162.1 3.3 %collective-permute-start.1 = (f32[2,8,6144]{2,1,0:T(8,128)}, f32[2,8,6144]{2,1,0:T(8,128)S(1)}, u32[]{:S(2)}, u32[]{:S(2)}) collective-permute-start(f32[2,8,6144]{2,1,0:T(8,128)} %get-tuple-element.5), channel_id=1, source_target_pairs={{0,1},{1,2},{2,3},{3,4},{4,5},{5,6},{6,7},{7,8},{8,9},{9,10},{10,1... | collective-permute-start | bytes 1179656 | tf_op jit(solution)/shard_map/ppermute | solution.py:73
  165.5 1.9 collective-permute-start.2
  168.2 30.7 %collective-permute-done.1.above = f32[2,8,6144]{2,1,0:T(8,128)S(1)} collective-permute-done((f32[2,8,6144]{2,1,0:T(8,128)}, f32[2,8,6144]{2,1,0:T(8,128)S(1)}, u32[]{:S(2)}, u32[]{:S(2)}) %collective-permute-start.1) | collective-permute-done | bytes 393248 | tf_op jit(solution)/shard_map/ppermute | solution.py:73
  200.5 1.9 copy-done.3
  202.4 4.1 %shard_map.192 = f32[2,64,6144]{2,1,0:T(8,128)} custom-call(s32[2,12,2]{2,1,0:T(8,128)S(1)} %copy.20.shifts, f32[2,64,6144]{2,1,0:T(8,128)S(1)} %copy-done.3, f32[2,8,6144]{2,1,0:T(8,128)S(1)} %collective-permute-done.1.above, f32[2,8,6144]{2,1,0:T(8,128)} %collective-permute-done.2.below), custom_call_target="tpu_custom_call" | custom-call | flops 15728640 | bytes 6291456 | tf_op jit(solution)/shard_map/pallas_call | solution.py:77
  208.6 5.5 %shard_map.191 = f32[2,64,6144]{2,1,0:T(8,128)} custom-call(f32[48,64,128]{2,1,0:T(8,128)S(1)} %bitcast.15, f32[48,64,128]{2,1,0:T(8,128)} %bitcast.7.refs_1_, bf16[512,512]{1,0:T(8,128)(2,1)S(1)} %copy-done.10, bf16[512,512]{1,0:T(8,128)(2,1)S(1)} %copy-done.11), custom_call_target="tpu_custom_call" | custom-call | tf_op jit(solution)/shard_map/pallas_call | solution.py:323
  (48 shorter events, 21.2 us)
Async XLA Ops:
  0.6 1.4 copy-start
  0.6 1.5 copy-start.4
  0.7 1.6 copy-start.5
  2.3 9.0 %copy-start.16 = (s32[12,2]{0,1:T(2,128)S(1)}, s32[12,2]{0,1:T(2,128)}, u32[]{:S(2)}) copy-start(s32[12,2]{0,1:T(2,128)} %param.20) | copy-start | bytes 292
  4.8 25.8 %all-to-all-start.1 = ((f32[16,3,32,128]{3,2,1,0:T(8,128)}), f32[16,3,32,128]{3,2,1,0:T(8,128)S(1)}, u32[]{:S(2)}, u32[]{:S(2)}) async-start(f32[16,3,32,128]{3,2,1,0:T(8,128)} %bitcast.4), calls=%async_computation.1 | async-start | bytes 1572864 | tf_op jit(solution)/shard_map/all_to_all | solution.py:363
  11.4 1.9 copy-start.1
  30.6 41.2 %all-to-all-start = ((f32[16,3,64,128]{3,2,1,0:T(8,128)}), f32[16,3,64,128]{3,2,1,0:T(8,128)}, u32[]{:S(2)}, u32[]{:S(2)}) async-start(f32[16,3,64,128]{3,2,1,0:T(8,128)} %bitcast.2), calls=%async_computation | async-start | bytes 3145728 | tf_op jit(solution)/shard_map/all_to_all | solution.py:363
  35.5 18.9 %collective-permute-start = (f32[16,3,32,128]{3,2,1,0:T(8,128)S(1)}, f32[16,3,32,128]{3,2,1,0:T(8,128)}, u32[]{:S(2)}, u32[]{:S(2)}) collective-permute-start(f32[16,3,32,128]{3,2,1,0:T(8,128)S(1)} %all-to-all-done.1), channel_id=1, source_target_pairs={{0,16},{16,0},{1,17},{17,1},{2,18},{18,2},{3,19},{19,3},{4,20},{20... | collective-permute-start | bytes 2359304 | tf_op jit(solution)/shard_map/ppermute | solution.py:371
  35.8 1.9 copy-start.2
  54.4 2.4 %copy-start.12 = (bf16[2048,1024]{1,0:T(8,128)(2,1)S(1)}, bf16[2048,1024]{1,0:T(8,128)(2,1)}, u32[]{:S(2)}) copy-start(bf16[2048,1024]{1,0:T(8,128)(2,1)} %constant.53.clone.table_high) | copy-start | bytes 12582916
  67.1 1.7 copy-start.13
  71.8 41.1 %all-to-all-start.3 = ((f32[16,3,64,128]{3,2,1,0:T(8,128)}), f32[16,3,64,128]{3,2,1,0:T(8,128)S(1)}, u32[]{:S(2)}, u32[]{:S(2)}) async-start(f32[16,3,64,128]{3,2,1,0:T(8,128)} %bitcast.6), calls=%async_computation.3 | async-start | bytes 3145728 | tf_op jit(solution)/shard_map/all_to_all | solution.py:363
  76.9 1.9 copy-start.14
  103.0 1.1 copy-start.9
  112.9 1.2 copy-start.7
  114.1 41.1 %all-to-all-start.2 = ((f32[16,3,64,128]{3,2,1,0:T(8,128)}), f32[16,3,64,128]{3,2,1,0:T(8,128)S(1)}, u32[]{:S(2)}, u32[]{:S(2)}) async-start(f32[16,3,64,128]{3,2,1,0:T(8,128)} %copy-done.9), calls=%async_computation.2 | async-start | bytes 3145728 | tf_op jit(solution)/shard_map/all_to_all | solution.py:384
  119.0 1.4 copy-start.8
  120.4 1.9 copy-start.15
  146.1 1.1 copy-start.6
  155.2 51.3 %all-to-all-start.4 = ((f32[16,3,64,128]{3,2,1,0:T(8,128)}), f32[16,3,64,128]{3,2,1,0:T(8,128)}, u32[]{:S(2)}, u32[]{:S(2)}) async-start(f32[16,3,64,128]{3,2,1,0:T(8,128)} %copy-done.6), calls=%async_computation.4 | async-start | bytes 3145728 | tf_op jit(solution)/shard_map/all_to_all | solution.py:384
  162.1 36.8 %collective-permute-start.1 = (f32[2,8,6144]{2,1,0:T(8,128)}, f32[2,8,6144]{2,1,0:T(8,128)S(1)}, u32[]{:S(2)}, u32[]{:S(2)}) collective-permute-start(f32[2,8,6144]{2,1,0:T(8,128)} %get-tuple-element.5), channel_id=1, source_target_pairs={{0,1},{1,2},{2,3},{3,4},{4,5},{5,6},{6,7},{7,8},{8,9},{9,10},{10,1... | collective-permute-start | bytes 1179656 | tf_op jit(solution)/shard_map/ppermute | solution.py:73
  165.5 35.0 %collective-permute-start.2 = (f32[2,8,6144]{2,1,0:T(8,128)}, f32[2,8,6144]{2,1,0:T(8,128)}, u32[]{:S(2)}, u32[]{:S(2)}) collective-permute-start(f32[2,8,6144]{2,1,0:T(8,128)} %get-tuple-element.4), channel_id=1, source_target_pairs={{1,0},{2,1},{3,2},{4,3},{5,4},{6,5},{7,6},{8,7},{9,8},{10,9},{11,1... | collective-permute-start | bytes 1179656 | tf_op jit(solution)/shard_map/ppermute | solution.py:74
  200.5 1.9 copy-start.3
  206.5 1.0 copy-start.10
  (1 other events, 1.0 us)
where the time goes:
time: 215 us; the launch traced here: 214 us
  waiting for transfers between devices  80 us (37%)
  Pallas kernels  76.4 us (36%)
  starting transfers between devices  31.7 us (15%)
  local copies, waits for them, and re-layouts  23.4 us (11%)
    pallas_call x2, Pallas kernels, kernel_products(): call(*column_parts(), block, plane_both, lanes)  48 us
    ppermute x1, waiting for transfers between devices, aligned(): above = lax.ppermute(tail, 'rows', [(i, i + 1) for i in range(count - 1)])  30.7 us
    all_to_all x3, waiting for transfers between devices, to_columns(): return lax.all_to_all(sent, 'rows', split_axis=0, concat_axis=0, tiled=True)  26 us
    unnamed x36, local copies, waits for them, and re-layouts  21.2 us
    all_to_all x3, starting transfers between devices, to_columns(): return lax.all_to_all(sent, 'rows', split_axis=0, concat_axis=0, tiled=True)  16.4 us
    ppermute x1, waiting for transfers between devices, per_device(): other = lax.ppermute(mine, 'group', [(0, 1), (1, 0)])  13.7 us
    pallas_call x1, Pallas kernels, kernel_plane(): pl.pallas_call(forward_halves, out_shape=jax.ShapeDtypeStruct((2 * F1, br...  10.3 us
    all_to_all x2, starting transfers between devices, per_device(): lax.all_to_all(block, 'rows', split_axis=0, concat_axis=0, tiled=True)  9.82 us
  transfers between devices with their start and end apart: 8, of which 7 were waited for; matrix products, arithmetic and copies ran while one was open for 2% of the time, Pallas kernels for 32%

commit v1 on v0

--- a/solution.py
+++ b/solution.py
@@ -331,6 +331,488 @@
     )(*blocks, *split_table(table))
 
 
+FOLD = F1 // 2
+TILE_GROUPS = TF2 // LANES
+BLOCK = 256
+STRIP = 64
+MESH_ID = pl.DeviceIdType.MESH
+
+
+def folded_table():
+    cosine, sine = trig(FOLD, F1, F1)
+    sine[0] = np.where(np.arange(F1) % 2 == 0, 1.0, -1.0)
+    return np.concatenate([cosine, sine])
+
+
+def swapped(values):
+    return pltpu.roll(values, LANES // 2, 1)
+
+
+def whole_kernel(
+    edges,
+    shifts,
+    spectra,
+    plane,
+    row_high_in,
+    row_low_in,
+    col_high_in,
+    col_low_in,
+    back_high_in,
+    back_low_in,
+    last_high_in,
+    last_low_in,
+    correlation,
+    aligned_out,
+    row_high,
+    row_low,
+    col_high,
+    col_low,
+    back_high,
+    back_low,
+    last_high,
+    last_low,
+    padded,
+    plane_rows,
+    plane_sent,
+    plane_got,
+    sent,
+    got,
+    returned,
+    bins,
+    coefs,
+    both,
+    high,
+    low,
+    pair_high,
+    pair_low,
+    load_sem,
+    halo_send,
+    halo_got,
+    plane_send_sem,
+    plane_got_sem,
+    swap_send_sem,
+    swap_got_sem,
+    spec_send_sem,
+    spec_got_sem,
+    back_send_sem,
+    back_got_sem,
+):
+    number, height, breadth = spectra.shape
+    count = lax.axis_size("rows")
+    chunks = breadth // LANES // count
+    per_chunk = count // TILE_GROUPS
+    share = plane_rows.shape[0]
+    me = lax.axis_index("rows")
+    side = lax.axis_index("group")
+    other = 1 - side
+    middle = slice(LANES, LANES + breadth)
+
+    def load(source, target, sem):
+        copy = pltpu.make_async_copy(source, target, load_sem.at[sem])
+        copy.start()
+        return copy
+
+    own = pl.ds(pl.multiple_of(side * share, share), share)
+    loads = [
+        load(plane.at[own], plane_rows, 0),
+        load(row_high_in, row_high, 1),
+        load(row_low_in, row_low, 2),
+        load(spectra, padded.at[:, pl.ds(MAXS, height), pl.ds(LANES, breadth)], 3),
+        load(col_high_in, col_high, 4),
+        load(col_low_in, col_low, 5),
+        load(back_high_in, back_high, 6),
+        load(back_low_in, back_low, 7),
+        load(last_high_in, last_high, 8),
+        load(last_low_in, last_low, 9),
+    ]
+
+    barrier = pltpu.get_barrier_semaphore()
+
+    def greet(step, carry):
+        peer = lax.rem(me + step, count)
+        pl.semaphore_signal(barrier, 1, device_id=(side, peer), device_id_type=MESH_ID)
+        return carry
+
+    lax.fori_loop(1, count, greet, 0)
+    pl.semaphore_signal(barrier, 1, device_id=(other, me), device_id_type=MESH_ID)
+    pl.semaphore_wait(barrier, count)
+
+    def remote(source, target, send, got_sem, where):
+        return pltpu.make_async_remote_copy(
+            src_ref=source,
+            dst_ref=target,
+            send_sem=send,
+            recv_sem=got_sem,
+            device_id=where,
+            device_id_type=MESH_ID,
+        )
+
+    def halo_down():
+        return remote(
+            spectra.at[:, pl.ds(height - MAXS, MAXS)],
+            padded.at[:, pl.ds(0, MAXS), pl.ds(LANES, breadth)],
+            halo_send.at[0],
+            halo_got.at[0],
+            (side, lax.rem(me + 1, count)),
+        )
+
+    def halo_up():
+        return remote(
+            spectra.at[:, pl.ds(0, MAXS)],
+            padded.at[:, pl.ds(MAXS + height, MAXS), pl.ds(LANES, breadth)],
+            halo_send.at[1],
+            halo_got.at[1],
+            (side, lax.rem(me + count - 1, count)),
+        )
+
+    @pl.when(me < count - 1)
+    def _():
+        halo_down().start()
+
+    @pl.when(me > 0)
+    def _():
+        halo_up().start()
+
+    def far_first(step, carry, start):
+        half = lax.div(step + 1, 2)
+        offset = count // 2 + half * (1 - 2 * lax.rem(step, 2))
+        start(lax.rem(me + offset, count))
+        return carry
+
+    def to_all(start):
+        lax.fori_loop(0, count - 1, lambda step, carry: far_first(step, carry, start), 0)
+
+    loads[0].wait()
+    loads[1].wait()
+    loads[2].wait()
+    for chunk in range(chunks):
+
+        def bins_of(rows, table_high, table_low):
+            return product_of(rows, table_high[...], table_low[...])
+
+        tiles = [
+            plane_rows[:, start : start + TF2]
+            for start in range(chunk * per_chunk * TF2, (chunk + 1) * per_chunk * TF2, TF2)
+        ]
+        found = bins_of(jnp.concatenate(tiles, axis=0), row_high, row_low)
+        for tile in range(per_chunk):
+            for group in range(TILE_GROUPS):
+                plane_sent[chunk, tile * TILE_GROUPS + group] = found[
+                    tile * share : (tile + 1) * share, group * LANES : (group + 1) * LANES
+                ]
+        plane_got[chunk, me, own] = plane_sent[chunk, me]
+
+        def send_plane(peer):
+            remote(
+                plane_sent.at[chunk, peer],
+                plane_got.at[chunk, me, own],
+                plane_send_sem.at[chunk],
+                plane_got_sem.at[chunk],
+                (side, peer),
+            ).start()
+
+        to_all(send_plane)
+
+    loads[3].wait()
+    column = lax.broadcasted_iota(jnp.int32, (1, TF2), 1)
+    for chunk in range(chunks):
+
+        def spectrum_bins(spectrum, carry):
+            parts = []
+            for tile in range(chunk * per_chunk, (chunk + 1) * per_chunk):
+                inside = (column >= edges[tile, 0]) & (column < TF2 - edges[tile, 1])
+                keeper = jnp.where(inside, 1.0, 0.0).astype(jnp.float32)
+                lanes = slice(LANES + tile * TF2, LANES + (tile + 1) * TF2)
+                parts.append(padded[spectrum, MAXS : MAXS + height, lanes] * keeper)
+            found = product_of(jnp.concatenate(parts, axis=0), row_high[...], row_low[...])
+            for tile in range(per_chunk):
+                for group in range(TILE_GROUPS):
+                    sent[chunk, spectrum, tile * TILE_GROUPS + group] = found[
+                        tile * height : (tile + 1) * height, group * LANES : (group + 1) * LANES
+                    ]
+            got[chunk, spectrum, me] = sent[chunk, spectrum, me]
+
+            def send_spectrum(peer):
+                remote(
+                    sent.at[chunk, spectrum, peer],
+                    got.at[chunk, spectrum, me],
+                    spec_send_sem.at[chunk, spectrum],
+                    spec_got_sem.at[chunk, spectrum],
+                    (side, peer),
+                ).start()
+
+            to_all(send_spectrum)
+            return carry
+
+        lax.fori_loop(0, number, spectrum_bins, 0)
+
+    total = height + 2 * MAXS
+    margin = jnp.zeros((number, total, LANES), jnp.float32)
+    padded[:, :, :LANES] = margin
+    padded[:, :, LANES + breadth :] = margin
+    blank = jnp.zeros((number, MAXS, breadth), jnp.float32)
+
+    @pl.when(me == 0)
+    def _():
+        padded[:, :MAXS, middle] = blank
+
+    @pl.when(me == count - 1)
+    def _():
+        padded[:, MAXS + height :, middle] = blank
+
+    @pl.when(me > 0)
+    def _():
+        halo_down().wait_recv()
+
+    @pl.when(me < count - 1)
+    def _():
+        halo_up().wait_recv()
+
+    window = TF2 + 2 * LANES
+    for spectrum in range(number):
+
+        @pl.loop(0, breadth // TF2)
+        def _(tile):
+            down = shifts[spectrum, tile, 0]
+            right = shifts[spectrum, tile, 1]
+            start = pl.multiple_of(tile * TF2, TF2)
+            part = padded[spectrum, :, pl.ds(start, window)]
+            part = pltpu.roll(part, lax.rem(right + window, window), 1)[:, LANES : LANES + TF2]
+            part = pltpu.roll(part, lax.rem(down + total, total), 0)
+            aligned_out[spectrum, :, pl.ds(start, TF2)] = part[MAXS : MAXS + height]
+
+    def landed(buffer, sem):
+        fifteen = buffer.at[pl.ds(0, count - 1)]
+        pltpu.make_async_copy(fifteen, fifteen, sem).wait()
+
+    def swap_plane(chunk):
+        half = plane_got.at[chunk, :, own]
+        return remote(
+            half, half, swap_send_sem.at[chunk], swap_got_sem.at[chunk], (other, me)
+        )
+
+    for chunk in range(chunks):
+        landed(plane_sent.at[chunk], plane_got_sem.at[chunk])
+        swap_plane(chunk).start()
+
+    def transform(width):
+        @pl.loop(0, F1 // BLOCK)
+        def _(step):
+            rows = pl.ds(pl.multiple_of(step * BLOCK, BLOCK), BLOCK)
+            both[rows, :width] = product_3(
+                col_high, col_low, rows, high[:, :width], low[:, :width]
+            )
+
+    for load_index in range(4, 10):
+        loads[load_index].wait()
+
+    lane = lax.broadcasted_iota(jnp.int32, (STRIP, LANES), 1)
+    is_real = lane < LANES // 2
+    first_row = lax.broadcasted_iota(jnp.int32, (STRIP, LANES), 0) == 0
+    alone = (lax.rem(lane, LANES // 2) == 0) & (lax.rem(me, TILE_GROUPS) == 0)
+
+    def strips(body):
+        @pl.loop(0, FOLD // STRIP)
+        def _(step):
+            start = pl.multiple_of(step * STRIP, STRIP)
+            body(pl.ds(start, STRIP), pl.ds(FOLD + start, STRIP))
+
+    zero = jnp.zeros((STRIP, LANES), jnp.float32)
+
+    def plane_coefs(chunk):
+        def body(top, bottom):
+            c, s = both[top, :LANES], both[bottom, :LANES]
+            sc, ss = swapped(c), swapped(s)
+            c2, s2 = c + c, s + s
+            coefs[chunk, 0, top, :] = jnp.where(alone | is_real, c2, sc + sc)
+            coefs[chunk, 1, top, :] = jnp.where(alone, zero, jnp.where(is_real, sc + sc, -c2))
+            coefs[chunk, 2, top, :] = jnp.where(alone | is_real, s2, ss + ss)
+            coefs[chunk, 3, top, :] = jnp.where(alone, zero, jnp.where(is_real, ss + ss, -s2))
+
+        strips(body)
+
+    def store_pair(rows, lanes, values, high_ref, low_ref):
+        high_ref[rows, lanes], low_ref[rows, lanes] = split(values)
+
+    def pairs(chunk):
+        for spectrum in range(number):
+            lanes = slice(spectrum * LANES, (spectrum + 1) * LANES)
+
+            def take(top, bottom):
+                c, s = both[top, lanes], both[bottom, lanes]
+                sc, ss = swapped(c), swapped(s)
+                a, d = coefs[chunk, 0, top, :], coefs[chunk, 1, top, :]
+                f, b = coefs[chunk, 2, top, :], coefs[chunk, 3, top, :]
+                return c, s, sc, ss, a, d, f, b
+
+            def body(top, bottom):
+                c, s, sc, ss, a, d, f, b = take(top, bottom)
+                store_pair(top, lanes, (c * a + sc * d) + (s * f + ss * b), pair_high, pair_low)
+                store_pair(bottom, lanes, (s * a + ss * d) - (c * f + sc * b), pair_high, pair_low)
+
+            strips(body)
+            top, bottom = pl.ds(0, STRIP), pl.ds(FOLD, STRIP)
+            c, s, sc, ss, a, d, f, b = take(top, bottom)
+            zeroth = 0.5 * (c * a + sc * d)
+            nyquist = 0.5 * (s * f + ss * b)
+            first = (c * a + sc * d) + (s * f + ss * b)
+            second = (s * a + ss * d) - (c * f + sc * b)
+            store_pair(top, lanes, jnp.where(first_row, zeroth, first), pair_high, pair_low)
+            store_pair(bottom, lanes, jnp.where(first_row, nyquist, second), pair_high, pair_low)
+
+    def gather(block, lanes):
+        @pl.loop(0, count)
+        def _(source):
+            rows = pl.ds(pl.multiple_of(source * height, height), height)
+            high[rows, lanes], low[rows, lanes] = split(block[source])
+
+    for chunk in range(chunks):
+        swapped_half = plane_got.at[chunk, :, pl.ds(pl.multiple_of(other * share, share), share)]
+        pltpu.make_async_copy(swapped_half, swapped_half, swap_got_sem.at[chunk]).wait()
+        gather(plane_got.at[chunk], slice(0, LANES))
+        transform(LANES)
+        plane_coefs(chunk)
+
+    for chunk in range(chunks):
+        for spectrum in range(number):
+            landed(got.at[chunk, spectrum], spec_got_sem.at[chunk, spectrum])
+            gather(got.at[chunk, spectrum], slice(spectrum * LANES, (spectrum + 1) * LANES))
+        transform(number * LANES)
+        pairs(chunk)
+        held = BLOCK // height
+
+        def back(step, carry):
+            place = lax.rem(lax.div(me, held) + count // held // 2 + step, count // held)
+            rows = pl.ds(pl.multiple_of(place * BLOCK, BLOCK), BLOCK)
+            values = product_3(back_high, back_low, rows, pair_high[...], pair_low[...])
+            for spectrum in range(number):
+                for part in range(held):
+                    returned[chunk, spectrum, place * held + part] = values[
+                        part * height : (part + 1) * height,
+                        spectrum * LANES : (spectrum + 1) * LANES,
+                    ]
+
+            def send_back(index, inner):
+                spectrum = lax.div(index, held)
+                peer = place * held + lax.rem(index, held)
+
+                @pl.when(peer != me)
+                def _():
+                    remote(
+                        returned.at[chunk, spectrum, peer],
+                        bins.at[chunk, spectrum, me],
+                        back_send_sem.at[chunk, spectrum],
+                        back_got_sem.at[chunk, spectrum],
+                        (side, peer),
+                    ).start()
+
+                return inner
+
+            lax.fori_loop(0, number * held, send_back, 0)
+            return carry
+
+        lax.fori_loop(0, count // held, back, 0)
+        for spectrum in range(number):
+            bins[chunk, spectrum, me] = returned[chunk, spectrum, me]
+
+    for chunk in range(chunks):
+        for spectrum in range(number):
+            landed(bins.at[chunk, spectrum], back_got_sem.at[chunk, spectrum])
+            parts = [
+                jnp.concatenate(
+                    [
+                        bins[chunk, spectrum, tile * TILE_GROUPS + group]
+                        for group in range(TILE_GROUPS)
+                    ],
+                    axis=1,
+                )
+                for tile in range(per_chunk)
+            ]
+            values = product_of(jnp.concatenate(parts, axis=0), last_high[...], last_low[...])
+            for tile in range(per_chunk):
+                start = (chunk * per_chunk + tile) * TF2
+                correlation[spectrum, :, start : start + TF2] = values[
+                    tile * height : (tile + 1) * height
+                ]
+
+    for chunk in range(chunks):
+        landed(plane_sent.at[chunk], plane_send_sem.at[chunk])
+        swap_plane(chunk).wait_send()
+        for spectrum in range(number):
+            landed(sent.at[chunk, spectrum], spec_send_sem.at[chunk, spectrum])
+            landed(returned.at[chunk, spectrum], back_send_sem.at[chunk, spectrum])
+
+    @pl.when(me < count - 1)
+    def _():
+        halo_down().wait_send()
+
+    @pl.when(me > 0)
+    def _():
+        halo_up().wait_send()
+
+
+def kernel_whole(spectra, plane, interval_edges, tile_shifts, forward, inverse):
+    number, height, breadth = spectra.shape
+    count = lax.axis_size("rows")
+    share = height // lax.axis_size("group")
+    chunks = breadth // LANES // count
+    columns = folded_table()
+    tables = (
+        *split_table(forward),
+        *split_table(columns),
+        *split_table(np.ascontiguousarray(columns.T)),
+        *split_table(inverse),
+    )
+    small = pl.BlockSpec(memory_space=pltpu.SMEM)
+    far = pl.BlockSpec(memory_space=pl.ANY)
+    near = pl.BlockSpec(memory_space=pltpu.VMEM)
+    whole = jax.ShapeDtypeStruct(spectra.shape, jnp.float32)
+    breadths = (F1, number * LANES)
+    blocks = (chunks, number, count, height, LANES)
+    return pl.pallas_call(
+        whole_kernel,
+        out_shape=(whole, whole),
+        in_specs=[small, small] + [far] * (2 + len(tables)),
+        out_specs=(near, near),
+        scratch_shapes=[pltpu.VMEM(table.shape, jnp.bfloat16) for table in tables]
+        + [
+            pltpu.VMEM((number, height + 2 * MAXS, breadth + 2 * LANES), jnp.float32),
+            pltpu.VMEM((share, breadth), jnp.float32),
+            pltpu.VMEM((chunks, count, share, LANES), jnp.float32),
+            pltpu.VMEM((chunks, count, height, LANES), jnp.float32),
+            pltpu.VMEM(blocks, jnp.float32),
+            pltpu.VMEM(blocks, jnp.float32),
+            pltpu.VMEM(blocks, jnp.float32),
+            pltpu.VMEM(blocks, jnp.float32),
+            pltpu.VMEM((chunks, 4, FOLD, LANES), jnp.float32),
+            pltpu.VMEM(breadths, jnp.float32),
+            pltpu.VMEM(breadths, jnp.bfloat16),
+            pltpu.VMEM(breadths, jnp.bfloat16),
+            pltpu.VMEM(breadths, jnp.bfloat16),
+            pltpu.VMEM(breadths, jnp.bfloat16),
+            pltpu.SemaphoreType.DMA((10,)),
+            pltpu.SemaphoreType.DMA((2,)),
+            pltpu.SemaphoreType.DMA((2,)),
+            pltpu.SemaphoreType.DMA((chunks,)),
+            pltpu.SemaphoreType.DMA((chunks,)),
+            pltpu.SemaphoreType.DMA((chunks,)),
+            pltpu.SemaphoreType.DMA((chunks,)),
+            pltpu.SemaphoreType.DMA((chunks, number)),
+            pltpu.SemaphoreType.DMA((chunks, number)),
+            pltpu.SemaphoreType.DMA((chunks, number)),
+            pltpu.SemaphoreType.DMA((chunks, number)),
+        ],
+        compiler_params=pltpu.CompilerParams(
+            collective_id=0, has_side_effects=True, vmem_limit_bytes=48 * 2**20
+        ),
+        cost_estimate=pl.CostEstimate(
+            flops=2 * 3 * F1 * F1 * (2 * number + 2) * chunks * LANES,
+            bytes_accessed=16 * spectra.size,
+            transcendentals=0,
+        ),
+    )(interval_edges, tile_shifts, spectra, plane, *tables)
+
+
 def per_device(spectra, plane, interval_edges, tile_shifts):
     number, height, breadth = spectra.shape
     count = lax.axis_size("rows")
@@ -348,6 +830,9 @@
     cohorts = lax.axis_size("group")
     share = height // cohorts
     whole_tiles = width == LANES and share % 16 == 0
+    if whole_tiles and cohorts == 2 and height * count == F1 and count % groups == 0:
+        tables = (forward.reshape(TF2, TF2), inverse.reshape(TF2, TF2))
+        return kernel_whole(spectra, plane, interval_edges, tile_shifts, *tables)
 
     def to_columns(rows, index, kept, after=None):
         held = rows.shape[1]

time: 215 us -> 182 us (0.85)
  Pallas kernels: 76.4 us -> 167 us
  waiting for transfers between devices: 80 us -> 0 us
  starting transfers between devices: 31.7 us -> 0 us
  local copies, waits for them, and re-layouts: 23.4 us -> 14.4 us
    pallas_call x8 -> x1, Pallas kernels: 76.4 us -> 167 us  [kernel_whole(): pl.pallas_call(whole_kernel, out_shape=(whole, whole), in_specs=[small, s...]
    ppermute x3 -> x0, waiting for transfers between devices: 46 us -> none  [the longest x1 30.7 us: aligned(): above = lax.ppermute(tail, 'rows', [(i, i + 1) for i in range(count - 1)])]
    all_to_all x5 -> x0, waiting for transfers between devices: 33.9 us -> none  [the longest x3 26 us: to_columns(): return lax.all_to_all(sent, 'rows', split_axis=0, concat_axis=0, tiled=True)]
    all_to_all x5 -> x0, starting transfers between devices: 26.2 us -> none  [the longest x3 16.4 us: to_columns(): return lax.all_to_all(sent, 'rows', split_axis=0, concat_axis=0, tiled=True)]
    unnamed x36 -> x18, local copies, waits for them, and re-layouts: 21.2 us -> 14.4 us
    ppermute x3 -> x0, starting transfers between devices: 5.5 us -> none  [the longest x1 3.33 us: aligned(): above = lax.ppermute(tail, 'rows', [(i, i + 1) for i in range(count - 1)])]
  transfers between devices with their start and end apart: 8 -> 0, of which waited for: 7 -> 0; matrix products, arithmetic and copies ran while one was open for 2% -> 0% of each run, Pallas kernels for 32% -> 0%
where the time goes in v1:
time: 182 us
  Pallas kernels  167 us (92%)
  local copies, waits for them, and re-layouts  14.4 us (8%)
    pallas_call x1, Pallas kernels, kernel_whole(): pl.pallas_call(whole_kernel, out_shape=(whole, whole), in_specs=[small, s...  167 us
    unnamed x18, local copies, waits for them, and re-layouts  14.4 us

profile of v1, /device:TPU:15, one launch (start us, length us, event | category | flops | bytes accessed | tf_op | source)
XLA Modules:
  0.0 181.6 jit_solution(16487109648789091090)
XLA Ops:
  0.6 0.8 copy.14.edges
  1.4 0.8 copy.15.shifts
  2.2 0.0 copy-start
  2.2 1.4 copy-done
  3.6 0.0 copy-start.1
  3.6 1.6 copy-done.1
  5.2 0.0 copy-start.2
  5.2 1.0 copy-done.2
  6.2 0.0 copy-start.3
  6.2 1.0 copy-done.3
  7.3 0.0 copy-start.4
  7.3 1.0 copy-done.4
  8.3 0.0 copy-start.5
  8.3 1.0 copy-done.5
  9.3 166.5 %shard_map.131 = (f32[2,64,6144]{2,1,0:T(8,128)}, f32[2,64,6144]{2,1,0:T(8,128)}) custom-call(s32[12,2]{1,0:T(8,128)S(1)} %copy.14.edges, s32[2,12,2]{2,1,0:T(8,128)S(1)} %copy.15.shifts, f32[2,64,6144]{2,1,0:T(8,128)} %spectra.1, f32[64,6144]{1,0:T(8,128)S(1)} %copy-done, bf16[512,512]{1,0:T(8,128)(2,1)S(1)} %copy-done.5, bf16[512,512]{1,0:T(8,128)(2,1)S(1)} %copy-done.4, ...), custom_call_target="tpu_custom_call" | custom-call | flops 14495514624 | bytes 12582912 | tf_op jit(solution)/shard_map/pallas_call | solution.py:772
  175.9 0.0 copy-start.6
  175.9 4.0 %copy.18 = f32[2,64,6144]{2,1,0:T(8,128)} copy(f32[2,64,6144]{2,1,0:T(8,128)} %get-tuple-element.4) | data formatting | bytes 6291456
  179.9 0.0 copy-done.6
  179.9 1.7 copy.19
Async XLA Ops:
  2.2 1.4 copy-start
  3.6 1.6 copy-start.1
  5.2 1.0 copy-start.2
  6.2 1.0 copy-start.3
  7.3 1.0 copy-start.4
  8.3 1.0 copy-start.5
  175.9 4.0 %copy-start.6 = (f32[2,64,6144]{2,1,0:T(8,128)S(1)}, f32[2,64,6144]{2,1,0:T(8,128)}, u32[]{:S(2)}) copy-start(f32[2,64,6144]{2,1,0:T(8,128)} %get-tuple-element.5) | copy-start | bytes 9437188

commit v2 on v1

--- a/solution.py
+++ b/solution.py
@@ -348,9 +348,45 @@
     return pltpu.roll(values, LANES // 2, 1)
 
 
+def rows_of(bins, table_high, table_low, out, chunk):
+    count, height = bins.shape[:2]
+    tiles = count // TILE_GROUPS
+    parts = [
+        jnp.concatenate([bins[tile * TILE_GROUPS + group] for group in range(TILE_GROUPS)], axis=1)
+        for tile in range(tiles)
+    ]
+    values = product_of(jnp.concatenate(parts, axis=0), table_high[...], table_low[...])
+    for tile in range(tiles):
+        start = (chunk * tiles + tile) * TF2
+        out[:, start : start + TF2] = values[tile * height : (tile + 1) * height]
+
+
+def last_kernel(
+    aligned_in, done, bins, last_high, last_low, correlation, aligned_out, fresh, sems
+):
+    width = done.shape[2]
+    copies = [
+        pltpu.make_async_copy(done, correlation.at[:, :, pl.ds(0, width)], sems.at[0]),
+        pltpu.make_async_copy(aligned_in, aligned_out, sems.at[1]),
+    ]
+    for copy in copies:
+        copy.start()
+    for spectrum in range(bins.shape[0]):
+        rows_of(bins.at[spectrum], last_high, last_low, fresh.at[spectrum], 0)
+        copy = pltpu.make_async_copy(
+            fresh.at[spectrum],
+            correlation.at[spectrum, :, pl.ds(width, fresh.shape[2])],
+            sems.at[2 + spectrum],
+        )
+        copy.start()
+        copies.append(copy)
+    for copy in copies:
+        copy.wait()
+
+
 def whole_kernel(
-    edges,
-    shifts,
+    edges_in,
+    shifts_in,
     spectra,
     plane,
     row_high_in,
@@ -361,16 +397,19 @@
     back_low_in,
     last_high_in,
     last_low_in,
+    aligned_out,
     correlation,
-    aligned_out,
+    bins_last,
+    last_high,
+    last_low,
+    edges,
+    shifts,
     row_high,
     row_low,
     col_high,
     col_low,
     back_high,
     back_low,
-    last_high,
-    last_low,
     padded,
     plane_rows,
     plane_sent,
@@ -424,6 +463,8 @@
         load(back_low_in, back_low, 7),
         load(last_high_in, last_high, 8),
         load(last_low_in, last_low, 9),
+        load(edges_in, edges, 10),
+        load(shifts_in, shifts, 11),
     ]
 
     barrier = pltpu.get_barrier_semaphore()
@@ -514,13 +555,15 @@
         to_all(send_plane)
 
     loads[3].wait()
+    loads[10].wait()
+    loads[11].wait()
     column = lax.broadcasted_iota(jnp.int32, (1, TF2), 1)
     for chunk in range(chunks):
 
         def spectrum_bins(spectrum, carry):
             parts = []
             for tile in range(chunk * per_chunk, (chunk + 1) * per_chunk):
-                inside = (column >= edges[tile, 0]) & (column < TF2 - edges[tile, 1])
+                inside = (column >= edges[0, tile]) & (column < TF2 - edges[1, tile])
                 keeper = jnp.where(inside, 1.0, 0.0).astype(jnp.float32)
                 lanes = slice(LANES + tile * TF2, LANES + (tile + 1) * TF2)
                 parts.append(padded[spectrum, MAXS : MAXS + height, lanes] * keeper)
@@ -573,8 +616,8 @@
 
         @pl.loop(0, breadth // TF2)
         def _(tile):
-            down = shifts[spectrum, tile, 0]
-            right = shifts[spectrum, tile, 1]
+            down = shifts[spectrum, 0, tile]
+            right = shifts[spectrum, 1, tile]
             start = pl.multiple_of(tile * TF2, TF2)
             part = padded[spectrum, :, pl.ds(start, window)]
             part = pltpu.roll(part, lax.rem(right + window, window), 1)[:, LANES : LANES + TF2]
@@ -680,6 +723,7 @@
         transform(number * LANES)
         pairs(chunk)
         held = BLOCK // height
+        target = bins.at[chunk] if chunk < chunks - 1 else bins_last
 
         def back(step, carry):
             place = lax.rem(lax.div(me, held) + count // held // 2 + step, count // held)
@@ -700,7 +744,7 @@
                 def _():
                     remote(
                         returned.at[chunk, spectrum, peer],
-                        bins.at[chunk, spectrum, me],
+                        target.at[spectrum, me],
                         back_send_sem.at[chunk, spectrum],
                         back_got_sem.at[chunk, spectrum],
                         (side, peer),
@@ -713,27 +757,14 @@
 
         lax.fori_loop(0, count // held, back, 0)
         for spectrum in range(number):
-            bins[chunk, spectrum, me] = returned[chunk, spectrum, me]
-
-    for chunk in range(chunks):
+            target[spectrum, me] = returned[chunk, spectrum, me]
+
+    for chunk in range(chunks - 1):
         for spectrum in range(number):
             landed(bins.at[chunk, spectrum], back_got_sem.at[chunk, spectrum])
-            parts = [
-                jnp.concatenate(
-                    [
-                        bins[chunk, spectrum, tile * TILE_GROUPS + group]
-                        for group in range(TILE_GROUPS)
-                    ],
-                    axis=1,
-                )
-                for tile in range(per_chunk)
-            ]
-            values = product_of(jnp.concatenate(parts, axis=0), last_high[...], last_low[...])
-            for tile in range(per_chunk):
-                start = (chunk * per_chunk + tile) * TF2
-                correlation[spectrum, :, start : start + TF2] = values[
-                    tile * height : (tile + 1) * height
-                ]
+            rows_of(bins.at[chunk, spectrum], last_high, last_low, correlation.at[spectrum], chunk)
+    for spectrum in range(number):
+        landed(bins_last.at[spectrum], back_got_sem.at[chunks - 1, spectrum])
 
     for chunk in range(chunks):
         landed(plane_sent.at[chunk], plane_send_sem.at[chunk])
@@ -763,18 +794,30 @@
         *split_table(np.ascontiguousarray(columns.T)),
         *split_table(inverse),
     )
-    small = pl.BlockSpec(memory_space=pltpu.SMEM)
-    far = pl.BlockSpec(memory_space=pl.ANY)
+    far = pl.BlockSpec(memory_space=pltpu.HBM)
     near = pl.BlockSpec(memory_space=pltpu.VMEM)
-    whole = jax.ShapeDtypeStruct(spectra.shape, jnp.float32)
     breadths = (F1, number * LANES)
     blocks = (chunks, number, count, height, LANES)
-    return pl.pallas_call(
+    late = breadth // chunks
+    held = (
+        pltpu.VMEM(spectra.shape, jnp.float32),
+        pltpu.VMEM((number, height, breadth - late), jnp.float32),
+        pltpu.VMEM(blocks[1:], jnp.float32),
+        pltpu.VMEM((TF2, TF2), jnp.bfloat16),
+        pltpu.VMEM((TF2, TF2), jnp.bfloat16),
+    )
+    small = (interval_edges.T, tile_shifts.transpose(0, 2, 1))
+    large = [
+        pltpu.with_memory_space_constraint(value, pltpu.HBM)
+        for value in (*small, spectra, plane, *map(jnp.asarray, tables))
+    ]
+    halfway = pl.pallas_call(
         whole_kernel,
-        out_shape=(whole, whole),
-        in_specs=[small, small] + [far] * (2 + len(tables)),
-        out_specs=(near, near),
-        scratch_shapes=[pltpu.VMEM(table.shape, jnp.bfloat16) for table in tables]
+        out_shape=held,
+        in_specs=[far] * len(large),
+        out_specs=(near,) * len(held),
+        scratch_shapes=[pltpu.SMEM(value.shape, jnp.int32) for value in small]
+        + [pltpu.VMEM(table.shape, jnp.bfloat16) for table in tables[:6]]
         + [
             pltpu.VMEM((number, height + 2 * MAXS, breadth + 2 * LANES), jnp.float32),
             pltpu.VMEM((share, breadth), jnp.float32),
@@ -783,14 +826,14 @@
             pltpu.VMEM(blocks, jnp.float32),
             pltpu.VMEM(blocks, jnp.float32),
             pltpu.VMEM(blocks, jnp.float32),
-            pltpu.VMEM(blocks, jnp.float32),
+            pltpu.VMEM((chunks - 1,) + blocks[1:], jnp.float32),
             pltpu.VMEM((chunks, 4, FOLD, LANES), jnp.float32),
             pltpu.VMEM(breadths, jnp.float32),
             pltpu.VMEM(breadths, jnp.bfloat16),
             pltpu.VMEM(breadths, jnp.bfloat16),
             pltpu.VMEM(breadths, jnp.bfloat16),
             pltpu.VMEM(breadths, jnp.bfloat16),
-            pltpu.SemaphoreType.DMA((10,)),
+            pltpu.SemaphoreType.DMA((12,)),
             pltpu.SemaphoreType.DMA((2,)),
             pltpu.SemaphoreType.DMA((2,)),
             pltpu.SemaphoreType.DMA((chunks,)),
@@ -803,14 +846,26 @@
             pltpu.SemaphoreType.DMA((chunks, number)),
         ],
         compiler_params=pltpu.CompilerParams(
-            collective_id=0, has_side_effects=True, vmem_limit_bytes=48 * 2**20
+            collective_id=0, has_side_effects=True, vmem_limit_bytes=44 * 2**20
         ),
         cost_estimate=pl.CostEstimate(
             flops=2 * 3 * F1 * F1 * (2 * number + 2) * chunks * LANES,
             bytes_accessed=16 * spectra.size,
             transcendentals=0,
         ),
-    )(interval_edges, tile_shifts, spectra, plane, *tables)
+    )(*large)
+    whole = jax.ShapeDtypeStruct(spectra.shape, jnp.float32)
+    return pl.pallas_call(
+        last_kernel,
+        out_shape=(whole, whole),
+        in_specs=[near] * len(held),
+        out_specs=(pl.BlockSpec(memory_space=pltpu.HBM),) * 2,
+        scratch_shapes=[
+            pltpu.VMEM((number, height, late), jnp.float32),
+            pltpu.SemaphoreType.DMA((2 + number,)),
+        ],
+        compiler_params=pltpu.CompilerParams(vmem_limit_bytes=16 * 2**20),
+    )(*halfway)
 
 
 def per_device(spectra, plane, interval_edges, tile_shifts):

time: 182 us -> 166 us (0.912)
  local copies, waits for them, and re-layouts: 14.4 us -> 0 us
  Pallas kernels: 167 us -> 165 us
    unnamed x18 -> x0, local copies, waits for them, and re-layouts: 14.4 us -> none
    pallas_call x1 -> x2, Pallas kernels: 167 us -> 165 us  [the longest x1 162 us: kernel_whole(): pl.pallas_call(whole_kernel, out_shape=held, in_specs=[far] * len(large),...]
where the time goes in v2:
time: 166 us
  Pallas kernels  165 us (99%)
    pallas_call x1, Pallas kernels, kernel_whole(): pl.pallas_call(whole_kernel, out_shape=held, in_specs=[far] * len(large),...  162 us
    pallas_call x1, Pallas kernels, kernel_whole(): pl.pallas_call(last_kernel, out_shape=(whole, whole), in_specs=[near] * l...  3.36 us

profile of v2, /device:TPU:15, one launch (start us, length us, event | category | flops | bytes accessed | tf_op | source)
XLA Modules:
  0.0 166.1 jit_solution(13558396719146802673)
XLA Ops:
  0.6 162.1 %shard_map.131 = (f32[2,64,6144]{2,1,0:T(8,128)S(1)}, f32[2,64,4096]{2,1,0:T(8,128)S(1)}, f32[2,16,64,128]{3,2,1,0:T(8,128)S(1)}, bf16[512,512]{1,0:T(8,128)(2,1)S(1)}, bf16[512,512]{1,0:T(8,128)(2,1)S(1)}) custom-call(s32[2,12]{1,0:T(2,128)} %bitcast.3, s32[2,2,12]{2,1,0:T(2,128)} %bitcast.2, f32[2,64,6144]{2,1,0:T(8,128)} %spectra.1, f32[64,6144]{1,0:T(8,128)} %plane.1, ...), custom_call_target="tpu_custom_call" | custom-call | flops 14495514624 | bytes 12582912 | tf_op jit(solution)/shard_map/pallas_call | solution.py:814
  162.7 3.4 %shard_map.132 = (f32[2,64,6144]{2,1,0:T(8,128)}, f32[2,64,6144]{2,1,0:T(8,128)}) custom-call(f32[2,64,6144]{2,1,0:T(8,128)S(1)} %get-tuple-element.7.aligned_in, f32[2,64,4096]{2,1,0:T(8,128)S(1)} %get-tuple-element.8.done, f32[2,16,64,128]{3,2,1,0:T(8,128)S(1)} %get-tuple-element.9.bins, bf16[512,512]{1,0:T(8,128)(2,1)S(1)} %get-tuple-element.10.last_high, ...), custom_call_target="tpu_custom_call" | custom-call | tf_op jit(solution)/shard_map/pallas_call | solution.py:858

commit v3 on v2

--- a/solution.py
+++ b/solution.py
@@ -335,6 +335,7 @@
 TILE_GROUPS = TF2 // LANES
 BLOCK = 256
 STRIP = 64
+QUAD = 4
 MESH_ID = pl.DeviceIdType.MESH
 
 
@@ -362,24 +363,21 @@
 
 
 def last_kernel(
-    aligned_in, done, bins, last_high, last_low, correlation, aligned_out, fresh, sems
+    aligned_in, done, bins, ready, last_high, last_low, correlation, aligned_out, fresh, sems
 ):
-    width = done.shape[2]
+    width, late, last = done.shape[2], fresh.shape[1], bins.shape[0] - 1
     copies = [
-        pltpu.make_async_copy(done, correlation.at[:, :, pl.ds(0, width)], sems.at[0]),
-        pltpu.make_async_copy(aligned_in, aligned_out, sems.at[1]),
+        pltpu.make_async_copy(aligned_in, aligned_out, sems.at[0]),
+        pltpu.make_async_copy(done, correlation.at[:, :, pl.ds(0, width)], sems.at[1]),
+        pltpu.make_async_copy(
+            ready, correlation.at[pl.ds(0, last), :, pl.ds(width, late)], sems.at[2]
+        ),
+        pltpu.make_async_copy(fresh, correlation.at[last, :, pl.ds(width, late)], sems.at[3]),
     ]
-    for copy in copies:
+    for copy in copies[:3]:
         copy.start()
-    for spectrum in range(bins.shape[0]):
-        rows_of(bins.at[spectrum], last_high, last_low, fresh.at[spectrum], 0)
-        copy = pltpu.make_async_copy(
-            fresh.at[spectrum],
-            correlation.at[spectrum, :, pl.ds(width, fresh.shape[2])],
-            sems.at[2 + spectrum],
-        )
-        copy.start()
-        copies.append(copy)
+    rows_of(bins.at[last], last_high, last_low, fresh, 0)
+    copies[3].start()
     for copy in copies:
         copy.wait()
 
@@ -400,6 +398,7 @@
     aligned_out,
     correlation,
     bins_last,
+    fresh,
     last_high,
     last_low,
     edges,
@@ -427,6 +426,9 @@
     load_sem,
     halo_send,
     halo_got,
+    detour,
+    detour_send,
+    detour_got,
     plane_send_sem,
     plane_got_sem,
     swap_send_sem,
@@ -446,6 +448,16 @@
     other = 1 - side
     middle = slice(LANES, LANES + breadth)
 
+    barrier = pltpu.get_barrier_semaphore()
+
+    def greet(step, carry):
+        peer = lax.rem(me + step, count)
+        pl.semaphore_signal(barrier, 1, device_id=(side, peer), device_id_type=MESH_ID)
+        return carry
+
+    lax.fori_loop(1, count, greet, 0)
+    pl.semaphore_signal(barrier, 1, device_id=(other, me), device_id_type=MESH_ID)
+
     def load(source, target, sem):
         copy = pltpu.make_async_copy(source, target, load_sem.at[sem])
         copy.start()
@@ -467,17 +479,6 @@
         load(shifts_in, shifts, 11),
     ]
 
-    barrier = pltpu.get_barrier_semaphore()
-
-    def greet(step, carry):
-        peer = lax.rem(me + step, count)
-        pl.semaphore_signal(barrier, 1, device_id=(side, peer), device_id_type=MESH_ID)
-        return carry
-
-    lax.fori_loop(1, count, greet, 0)
-    pl.semaphore_signal(barrier, 1, device_id=(other, me), device_id_type=MESH_ID)
-    pl.semaphore_wait(barrier, count)
-
     def remote(source, target, send, got_sem, where):
         return pltpu.make_async_remote_copy(
             src_ref=source,
@@ -488,60 +489,185 @@
             device_id_type=MESH_ID,
         )
 
-    def halo_down():
+    last = number - 1
+    middle_low, middle_high = count // 2 - 1, count // 2
+    senders, takers = (middle_low, middle_high), (middle_high, middle_low)
+    detours = (middle_low - 2, middle_high + 2)
+    outside = pl.ds(0, MAXS), pl.ds(MAXS + height, MAXS)
+    inside_rows = pl.ds(height - MAXS, MAXS), pl.ds(0, MAXS)
+    has_next = (me < count - 1, me > 0)
+    has_previous = (me > 0, me < count - 1)
+
+    def halo(way, which):
+        kept = pl.ds(0, last) if which == 0 else pl.ds(last, 1)
+        peer = lax.rem(me + (1, count - 1)[way], count)
         return remote(
-            spectra.at[:, pl.ds(height - MAXS, MAXS)],
-            padded.at[:, pl.ds(0, MAXS), pl.ds(LANES, breadth)],
-            halo_send.at[0],
-            halo_got.at[0],
-            (side, lax.rem(me + 1, count)),
+            spectra.at[kept, inside_rows[way]],
+            padded.at[kept, outside[way], pl.ds(LANES, breadth)],
+            halo_send.at[way, which],
+            halo_got.at[way, which],
+            (side, peer),
         )
 
-    def halo_up():
+    def detour_out(way):
         return remote(
-            spectra.at[:, pl.ds(0, MAXS)],
-            padded.at[:, pl.ds(MAXS + height, MAXS), pl.ds(LANES, breadth)],
-            halo_send.at[1],
-            halo_got.at[1],
-            (side, lax.rem(me + count - 1, count)),
+            spectra.at[pl.ds(last, 1), inside_rows[way]],
+            detour.at[way],
+            halo_send.at[way, 1],
+            detour_got.at[way],
+            (side, detours[way]),
         )
 
-    @pl.when(me < count - 1)
-    def _():
-        halo_down().start()
-
-    @pl.when(me > 0)
-    def _():
-        halo_up().start()
-
-    def far_first(step, carry, start):
-        half = lax.div(step + 1, 2)
-        offset = count // 2 + half * (1 - 2 * lax.rem(step, 2))
-        start(lax.rem(me + offset, count))
-        return carry
+    def detour_on(way):
+        return remote(
+            detour.at[way],
+            padded.at[pl.ds(last, 1), outside[way], pl.ds(LANES, breadth)],
+            detour_send.at[way],
+            halo_got.at[way, 1],
+            (side, takers[way]),
+        )
+
+    def send_halos():
+        for way in range(2):
+            pl.when(has_next[way])(lambda: halo(way, 0).start())
+            pl.when(has_next[way] & (me != senders[way]))(lambda: halo(way, 1).start())
+            pl.when(me == senders[way])(lambda: detour_out(way).start())
+
+    def pass_halos():
+        for way in range(2):
+
+            @pl.when(me == detours[way])
+            def _():
+                detour_out(way).wait_recv()
+                detour_on(way).start()
+
+    def take_halos():
+        for way in range(2):
+            for which in range(2):
+                pl.when(has_previous[way])(lambda: halo(way, which).wait_recv())
+
+    def finish_halos():
+        for way in range(2):
+            for which in range(2):
+                pl.when(has_next[way])(lambda: halo(way, which).wait_send())
+            pl.when(me == detours[way])(lambda: detour_on(way).wait_send())
 
     def to_all(start):
-        lax.fori_loop(0, count - 1, lambda step, carry: far_first(step, carry, start), 0)
-
-    loads[0].wait()
-    loads[1].wait()
-    loads[2].wait()
-    for chunk in range(chunks):
-
-        def bins_of(rows, table_high, table_low):
-            return product_of(rows, table_high[...], table_low[...])
-
+        def one(step, carry):
+            half = lax.div(step + 1, 2)
+            offset = count // 2 + half * (1 - 2 * lax.rem(step, 2))
+            start(lax.rem(me + offset, count))
+            return carry
+
+        lax.fori_loop(0, count - 1, one, 0)
+
+    def to_all_last(start):
+        quad, place = lax.div(me, QUAD), lax.rem(me, QUAD)
+        across = 2 * (1 - lax.div(quad, 2))
+        for target in (across, across + 1, quad + 1 - 2 * lax.rem(quad, 2)):
+            for turn in range(QUAD):
+                start(target * QUAD + lax.rem(place + turn, QUAD))
+        for turn in range(1, QUAD):
+            start(quad * QUAD + lax.rem(place + turn, QUAD))
+
+    column = lax.broadcasted_iota(jnp.int32, (1, TF2), 1)
+    total = height + 2 * MAXS
+    window = TF2 + 2 * LANES
+
+    def landed(buffer, sem):
+        fifteen = buffer.at[pl.ds(0, count - 1)]
+        pltpu.make_async_copy(fifteen, fifteen, sem).wait()
+
+    def swap_plane(chunk):
+        half = plane_got.at[chunk, :, own]
+        return remote(
+            half, half, swap_send_sem.at[chunk], swap_got_sem.at[chunk], (other, me)
+        )
+
+    def transform(width):
+        @pl.loop(0, F1 // BLOCK)
+        def _(step):
+            rows = pl.ds(pl.multiple_of(step * BLOCK, BLOCK), BLOCK)
+            both[rows, :width] = product_3(
+                col_high, col_low, rows, high[:, :width], low[:, :width]
+            )
+
+    lane = lax.broadcasted_iota(jnp.int32, (STRIP, LANES), 1)
+    is_real = lane < LANES // 2
+    first_row = lax.broadcasted_iota(jnp.int32, (STRIP, LANES), 0) == 0
+    alone = (lax.rem(lane, LANES // 2) == 0) & (lax.rem(me, TILE_GROUPS) == 0)
+
+    def strips(body):
+        @pl.loop(0, FOLD // STRIP)
+        def _(step):
+            start = pl.multiple_of(step * STRIP, STRIP)
+            body(pl.ds(start, STRIP), pl.ds(FOLD + start, STRIP))
+
+    zero = jnp.zeros((STRIP, LANES), jnp.float32)
+
+    def plane_coefs(chunk):
+        def body(top, bottom):
+            c, s = both[top, :LANES], both[bottom, :LANES]
+            sc, ss = swapped(c), swapped(s)
+            c2, s2 = c + c, s + s
+            coefs[chunk, 0, top, :] = jnp.where(alone | is_real, c2, sc + sc)
+            coefs[chunk, 1, top, :] = jnp.where(alone, zero, jnp.where(is_real, sc + sc, -c2))
+            coefs[chunk, 2, top, :] = jnp.where(alone | is_real, s2, ss + ss)
+            coefs[chunk, 3, top, :] = jnp.where(alone, zero, jnp.where(is_real, ss + ss, -s2))
+
+        strips(body)
+
+    def store_pair(rows, lanes, values, high_ref, low_ref):
+        high_ref[rows, lanes], low_ref[rows, lanes] = split(values)
+
+    def pairs(chunk):
+        for spectrum in range(number):
+            lanes = slice(spectrum * LANES, (spectrum + 1) * LANES)
+
+            def take(top, bottom):
+                c, s = both[top, lanes], both[bottom, lanes]
+                sc, ss = swapped(c), swapped(s)
+                a, d = coefs[chunk, 0, top, :], coefs[chunk, 1, top, :]
+                f, b = coefs[chunk, 2, top, :], coefs[chunk, 3, top, :]
+                return c, s, sc, ss, a, d, f, b
+
+            def body(top, bottom):
+                c, s, sc, ss, a, d, f, b = take(top, bottom)
+                store_pair(top, lanes, (c * a + sc * d) + (s * f + ss * b), pair_high, pair_low)
+                store_pair(bottom, lanes, (s * a + ss * d) - (c * f + sc * b), pair_high, pair_low)
+
+            strips(body)
+            top, bottom = pl.ds(0, STRIP), pl.ds(FOLD, STRIP)
+            c, s, sc, ss, a, d, f, b = take(top, bottom)
+            zeroth = 0.5 * (c * a + sc * d)
+            nyquist = 0.5 * (s * f + ss * b)
+            first = (c * a + sc * d) + (s * f + ss * b)
+            second = (s * a + ss * d) - (c * f + sc * b)
+            store_pair(top, lanes, jnp.where(first_row, zeroth, first), pair_high, pair_low)
+            store_pair(bottom, lanes, jnp.where(first_row, nyquist, second), pair_high, pair_low)
+
+    def gather(block, lanes):
+        @pl.loop(0, count)
+        def _(source):
+            rows = pl.ds(pl.multiple_of(source * height, height), height)
+            high[rows, lanes], low[rows, lanes] = split(block[source])
+    held = BLOCK // height
+
+    def send_plane_bins(chunk):
         tiles = [
             plane_rows[:, start : start + TF2]
             for start in range(chunk * per_chunk * TF2, (chunk + 1) * per_chunk * TF2, TF2)
         ]
-        found = bins_of(jnp.concatenate(tiles, axis=0), row_high, row_low)
+        found = product_of(jnp.concatenate(tiles, axis=0), row_high[...], row_low[...])
         for tile in range(per_chunk):
             for group in range(TILE_GROUPS):
                 plane_sent[chunk, tile * TILE_GROUPS + group] = found[
                     tile * share : (tile + 1) * share, group * LANES : (group + 1) * LANES
                 ]
         plane_got[chunk, me, own] = plane_sent[chunk, me]
+
+        if chunk == 0:
+            pl.semaphore_wait(barrier, count)
 
         def send_plane(peer):
             remote(
@@ -554,12 +680,7 @@
 
         to_all(send_plane)
 
-    loads[3].wait()
-    loads[10].wait()
-    loads[11].wait()
-    column = lax.broadcasted_iota(jnp.int32, (1, TF2), 1)
-    for chunk in range(chunks):
-
+    def send_spectra_bins(chunk):
         def spectrum_bins(spectrum, carry):
             parts = []
             for tile in range(chunk * per_chunk, (chunk + 1) * per_chunk):
@@ -589,144 +710,54 @@
 
         lax.fori_loop(0, number, spectrum_bins, 0)
 
-    total = height + 2 * MAXS
-    margin = jnp.zeros((number, total, LANES), jnp.float32)
-    padded[:, :, :LANES] = margin
-    padded[:, :, LANES + breadth :] = margin
-    blank = jnp.zeros((number, MAXS, breadth), jnp.float32)
-
-    @pl.when(me == 0)
-    def _():
-        padded[:, :MAXS, middle] = blank
-
-    @pl.when(me == count - 1)
-    def _():
-        padded[:, MAXS + height :, middle] = blank
-
-    @pl.when(me > 0)
-    def _():
-        halo_down().wait_recv()
-
-    @pl.when(me < count - 1)
-    def _():
-        halo_up().wait_recv()
-
-    window = TF2 + 2 * LANES
-    for spectrum in range(number):
-
-        @pl.loop(0, breadth // TF2)
-        def _(tile):
-            down = shifts[spectrum, 0, tile]
-            right = shifts[spectrum, 1, tile]
-            start = pl.multiple_of(tile * TF2, TF2)
-            part = padded[spectrum, :, pl.ds(start, window)]
-            part = pltpu.roll(part, lax.rem(right + window, window), 1)[:, LANES : LANES + TF2]
-            part = pltpu.roll(part, lax.rem(down + total, total), 0)
-            aligned_out[spectrum, :, pl.ds(start, TF2)] = part[MAXS : MAXS + height]
-
-    def landed(buffer, sem):
-        fifteen = buffer.at[pl.ds(0, count - 1)]
-        pltpu.make_async_copy(fifteen, fifteen, sem).wait()
-
-    def swap_plane(chunk):
-        half = plane_got.at[chunk, :, own]
-        return remote(
-            half, half, swap_send_sem.at[chunk], swap_got_sem.at[chunk], (other, me)
-        )
-
-    for chunk in range(chunks):
+    def align():
+        margin = jnp.zeros((number, total, LANES), jnp.float32)
+        padded[:, :, :LANES] = margin
+        padded[:, :, LANES + breadth :] = margin
+        blank = jnp.zeros((number, MAXS, breadth), jnp.float32)
+
+        @pl.when(me == 0)
+        def _():
+            padded[:, :MAXS, middle] = blank
+
+        @pl.when(me == count - 1)
+        def _():
+            padded[:, MAXS + height :, middle] = blank
+
+
+        for spectrum in range(number):
+
+            @pl.loop(0, breadth // TF2)
+            def _(tile):
+                down = shifts[spectrum, 0, tile]
+                right = shifts[spectrum, 1, tile]
+                start = pl.multiple_of(tile * TF2, TF2)
+                part = padded[spectrum, :, pl.ds(start, window)]
+                part = pltpu.roll(part, lax.rem(right + window, window), 1)[:, LANES : LANES + TF2]
+                part = pltpu.roll(part, lax.rem(down + total, total), 0)
+                aligned_out[spectrum, :, pl.ds(start, TF2)] = part[MAXS : MAXS + height]
+
+    def exchange_plane(chunk):
         landed(plane_sent.at[chunk], plane_got_sem.at[chunk])
         swap_plane(chunk).start()
 
-    def transform(width):
-        @pl.loop(0, F1 // BLOCK)
-        def _(step):
-            rows = pl.ds(pl.multiple_of(step * BLOCK, BLOCK), BLOCK)
-            both[rows, :width] = product_3(
-                col_high, col_low, rows, high[:, :width], low[:, :width]
-            )
-
-    for load_index in range(4, 10):
-        loads[load_index].wait()
-
-    lane = lax.broadcasted_iota(jnp.int32, (STRIP, LANES), 1)
-    is_real = lane < LANES // 2
-    first_row = lax.broadcasted_iota(jnp.int32, (STRIP, LANES), 0) == 0
-    alone = (lax.rem(lane, LANES // 2) == 0) & (lax.rem(me, TILE_GROUPS) == 0)
-
-    def strips(body):
-        @pl.loop(0, FOLD // STRIP)
-        def _(step):
-            start = pl.multiple_of(step * STRIP, STRIP)
-            body(pl.ds(start, STRIP), pl.ds(FOLD + start, STRIP))
-
-    zero = jnp.zeros((STRIP, LANES), jnp.float32)
-
-    def plane_coefs(chunk):
-        def body(top, bottom):
-            c, s = both[top, :LANES], both[bottom, :LANES]
-            sc, ss = swapped(c), swapped(s)
-            c2, s2 = c + c, s + s
-            coefs[chunk, 0, top, :] = jnp.where(alone | is_real, c2, sc + sc)
-            coefs[chunk, 1, top, :] = jnp.where(alone, zero, jnp.where(is_real, sc + sc, -c2))
-            coefs[chunk, 2, top, :] = jnp.where(alone | is_real, s2, ss + ss)
-            coefs[chunk, 3, top, :] = jnp.where(alone, zero, jnp.where(is_real, ss + ss, -s2))
-
-        strips(body)
-
-    def store_pair(rows, lanes, values, high_ref, low_ref):
-        high_ref[rows, lanes], low_ref[rows, lanes] = split(values)
-
-    def pairs(chunk):
-        for spectrum in range(number):
-            lanes = slice(spectrum * LANES, (spectrum + 1) * LANES)
-
-            def take(top, bottom):
-                c, s = both[top, lanes], both[bottom, lanes]
-                sc, ss = swapped(c), swapped(s)
-                a, d = coefs[chunk, 0, top, :], coefs[chunk, 1, top, :]
-                f, b = coefs[chunk, 2, top, :], coefs[chunk, 3, top, :]
-                return c, s, sc, ss, a, d, f, b
-
-            def body(top, bottom):
-                c, s, sc, ss, a, d, f, b = take(top, bottom)
-                store_pair(top, lanes, (c * a + sc * d) + (s * f + ss * b), pair_high, pair_low)
-                store_pair(bottom, lanes, (s * a + ss * d) - (c * f + sc * b), pair_high, pair_low)
-
-            strips(body)
-            top, bottom = pl.ds(0, STRIP), pl.ds(FOLD, STRIP)
-            c, s, sc, ss, a, d, f, b = take(top, bottom)
-            zeroth = 0.5 * (c * a + sc * d)
-            nyquist = 0.5 * (s * f + ss * b)
-            first = (c * a + sc * d) + (s * f + ss * b)
-            second = (s * a + ss * d) - (c * f + sc * b)
-            store_pair(top, lanes, jnp.where(first_row, zeroth, first), pair_high, pair_low)
-            store_pair(bottom, lanes, jnp.where(first_row, nyquist, second), pair_high, pair_low)
-
-    def gather(block, lanes):
-        @pl.loop(0, count)
-        def _(source):
-            rows = pl.ds(pl.multiple_of(source * height, height), height)
-            high[rows, lanes], low[rows, lanes] = split(block[source])
-
-    for chunk in range(chunks):
+    def transform_plane(chunk):
         swapped_half = plane_got.at[chunk, :, pl.ds(pl.multiple_of(other * share, share), share)]
         pltpu.make_async_copy(swapped_half, swapped_half, swap_got_sem.at[chunk]).wait()
         gather(plane_got.at[chunk], slice(0, LANES))
         transform(LANES)
         plane_coefs(chunk)
 
-    for chunk in range(chunks):
+    def multiply(chunk):
         for spectrum in range(number):
             landed(got.at[chunk, spectrum], spec_got_sem.at[chunk, spectrum])
             gather(got.at[chunk, spectrum], slice(spectrum * LANES, (spectrum + 1) * LANES))
         transform(number * LANES)
         pairs(chunk)
-        held = BLOCK // height
         target = bins.at[chunk] if chunk < chunks - 1 else bins_last
 
         def back(step, carry):
-            place = lax.rem(lax.div(me, held) + count // held // 2 + step, count // held)
+            place = step
             rows = pl.ds(pl.multiple_of(place * BLOCK, BLOCK), BLOCK)
             values = product_3(back_high, back_low, rows, pair_high[...], pair_low[...])
             for spectrum in range(number):
@@ -736,35 +767,56 @@
                         spectrum * LANES : (spectrum + 1) * LANES,
                     ]
 
-            def send_back(index, inner):
-                spectrum = lax.div(index, held)
-                peer = place * held + lax.rem(index, held)
-
-                @pl.when(peer != me)
-                def _():
-                    remote(
-                        returned.at[chunk, spectrum, peer],
-                        target.at[spectrum, me],
-                        back_send_sem.at[chunk, spectrum],
-                        back_got_sem.at[chunk, spectrum],
-                        (side, peer),
-                    ).start()
-
-                return inner
-
-            lax.fori_loop(0, number * held, send_back, 0)
             return carry
 
         lax.fori_loop(0, count // held, back, 0)
         for spectrum in range(number):
+
+            def send_back(peer):
+                remote(
+                    returned.at[chunk, spectrum, peer],
+                    target.at[spectrum, me],
+                    back_send_sem.at[chunk, spectrum],
+                    back_got_sem.at[chunk, spectrum],
+                    (side, peer),
+                ).start()
+
+            (to_all if chunk < chunks - 1 else to_all_last)(send_back)
             target[spectrum, me] = returned[chunk, spectrum, me]
 
-    for chunk in range(chunks - 1):
+    def finish_rows(chunk):
         for spectrum in range(number):
             landed(bins.at[chunk, spectrum], back_got_sem.at[chunk, spectrum])
             rows_of(bins.at[chunk, spectrum], last_high, last_low, correlation.at[spectrum], chunk)
+
+    for load_index in (0, 1, 2):
+        loads[load_index].wait()
+    for chunk in range(chunks):
+        send_plane_bins(chunk)
+    for load_index in (3, 10, 11):
+        loads[load_index].wait()
+    send_spectra_bins(0)
+    for chunk in range(chunks):
+        exchange_plane(chunk)
+    for chunk in range(1, chunks):
+        send_spectra_bins(chunk)
+        if chunk == 1:
+            send_halos()
+    for load_index in range(4, 10):
+        loads[load_index].wait()
+    for chunk in range(chunks):
+        transform_plane(chunk)
+    pass_halos()
+    for chunk in range(chunks):
+        multiply(chunk)
+    take_halos()
+    align()
+    for chunk in range(chunks - 1):
+        finish_rows(chunk)
     for spectrum in range(number):
         landed(bins_last.at[spectrum], back_got_sem.at[chunks - 1, spectrum])
+        if spectrum < number - 1:
+            rows_of(bins_last.at[spectrum], last_high, last_low, fresh.at[spectrum], 0)
 
     for chunk in range(chunks):
         landed(plane_sent.at[chunk], plane_send_sem.at[chunk])
@@ -773,14 +825,7 @@
             landed(sent.at[chunk, spectrum], spec_send_sem.at[chunk, spectrum])
             landed(returned.at[chunk, spectrum], back_send_sem.at[chunk, spectrum])
 
-    @pl.when(me < count - 1)
-    def _():
-        halo_down().wait_send()
-
-    @pl.when(me > 0)
-    def _():
-        halo_up().wait_send()
-
+    finish_halos()
 
 def kernel_whole(spectra, plane, interval_edges, tile_shifts, forward, inverse):
     number, height, breadth = spectra.shape
@@ -803,6 +848,7 @@
         pltpu.VMEM(spectra.shape, jnp.float32),
         pltpu.VMEM((number, height, breadth - late), jnp.float32),
         pltpu.VMEM(blocks[1:], jnp.float32),
+        pltpu.VMEM((number - 1, height, late), jnp.float32),
         pltpu.VMEM((TF2, TF2), jnp.bfloat16),
         pltpu.VMEM((TF2, TF2), jnp.bfloat16),
     )
@@ -834,6 +880,9 @@
             pltpu.VMEM(breadths, jnp.bfloat16),
             pltpu.VMEM(breadths, jnp.bfloat16),
             pltpu.SemaphoreType.DMA((12,)),
+            pltpu.SemaphoreType.DMA((2, 2)),
+            pltpu.SemaphoreType.DMA((2, 2)),
+            pltpu.VMEM((2, 1, MAXS, breadth), jnp.float32),
             pltpu.SemaphoreType.DMA((2,)),
             pltpu.SemaphoreType.DMA((2,)),
             pltpu.SemaphoreType.DMA((chunks,)),
@@ -861,8 +910,8 @@
         in_specs=[near] * len(held),
         out_specs=(pl.BlockSpec(memory_space=pltpu.HBM),) * 2,
         scratch_shapes=[
-            pltpu.VMEM((number, height, late), jnp.float32),
-            pltpu.SemaphoreType.DMA((2 + number,)),
+            pltpu.VMEM((height, late), jnp.float32),
+            pltpu.SemaphoreType.DMA((4,)),
         ],
         compiler_params=pltpu.CompilerParams(vmem_limit_bytes=16 * 2**20),
     )(*halfway)
@@ -885,7 +934,7 @@
     cohorts = lax.axis_size("group")
     share = height // cohorts
     whole_tiles = width == LANES and share % 16 == 0
-    if whole_tiles and cohorts == 2 and height * count == F1 and count % groups == 0:
+    if whole_tiles and cohorts == 2 and height * count == F1 and count == QUAD * QUAD and number > 1:
         tables = (forward.reshape(TF2, TF2), inverse.reshape(TF2, TF2))
         return kernel_whole(spectra, plane, interval_edges, tile_shifts, *tables)
 

time: 166 us -> 164 us (0.988)
  Pallas kernels: 165 us -> 162 us
    pallas_call x1, Pallas kernels: 162 us -> 160 us  [kernel_whole(): pl.pallas_call(whole_kernel, out_shape=held, in_specs=[far] * len(large),...]
where the time goes in v3:
time: 164 us; the launch traced here: 163 us
  Pallas kernels  162 us (99%)
    pallas_call x1, Pallas kernels, kernel_whole(): pl.pallas_call(whole_kernel, out_shape=held, in_specs=[far] * len(large),...  160 us

profile of v3, /device:TPU:15, one launch (start us, length us, event | category | flops | bytes accessed | tf_op | source)
XLA Modules:
  0.0 162.9 jit_solution(11331885452599883451)
XLA Ops:
  0.6 159.6 %shard_map.131 = (f32[2,64,6144]{2,1,0:T(8,128)S(1)}, f32[2,64,4096]{2,1,0:T(8,128)S(1)}, f32[2,16,64,128]{3,2,1,0:T(8,128)S(1)}, f32[1,64,2048]{2,1,0:T(8,128)S...) custom-call(s32[2,12]{1,0:T(2,128)} %bitcast.3, s32[2,2,12]{2,1,0:T(2,128)} %bitcast.2, ...), custom_call_target="tpu_custom_call" | custom-call | flops 14495514624 | bytes 12582912 | tf_op jit(solution)/shard_map/pallas_call | solution.py:860
  160.2 2.7 %shard_map.132 = (f32[2,64,6144]{2,1,0:T(8,128)}, f32[2,64,6144]{2,1,0:T(8,128)}) custom-call(f32[2,64,6144]{2,1,0:T(8,128)S(1)} %get-tuple-element.8.aligned_in, f32[2,64,4096]{2,1,0:T(8,128)S(1)} %get-tuple-element.9.done, f32[2,16,64,128]{3,2,1,0:T(8,128)S(1)} %get-tuple-element.10.bins, f32[1,64,2048]{2,1,0:T(8,128)S(1)} %get-tuple-element.11.ready, ...), custom_call_target="tpu_custom_call" | custom-call | tf_op jit(solution)/shard_map/pallas_call | solution.py:907

commit v4 on v3

--- a/solution.py
+++ b/solution.py
@@ -374,8 +374,8 @@
         ),
         pltpu.make_async_copy(fresh, correlation.at[last, :, pl.ds(width, late)], sems.at[3]),
     ]
-    for copy in copies[:3]:
-        copy.start()
+    for place, copy in enumerate(copies[:3]):
+        copy.start(priority=place % 2)
     rows_of(bins.at[last], last_high, last_low, fresh, 0)
     copies[3].start()
     for copy in copies:

time: 164 us -> 164 us (level)
  no operation moved by 1% of the time
where the time goes in v4:
time: 164 us; the launch traced here: 163 us
  Pallas kernels  162 us (99%)
    pallas_call x1, Pallas kernels, kernel_whole(): pl.pallas_call(whole_kernel, out_shape=held, in_specs=[far] * len(large),...  160 us

profile of v4, /device:TPU:15, one launch (start us, length us, event | category | flops | bytes accessed | tf_op | source)
XLA Modules:
  0.0 162.9 jit_solution(2111967655948771552)
XLA Ops:
  0.6 159.6 %shard_map.131 = (f32[2,64,6144]{2,1,0:T(8,128)S(1)}, f32[2,64,4096]{2,1,0:T(8,128)S(1)}, f32[2,16,64,128]{3,2,1,0:T(8,128)S(1)}, f32[1,64,2048]{2,1,0:T(8,128)S...) custom-call(s32[2,12]{1,0:T(2,128)} %bitcast.3, s32[2,2,12]{2,1,0:T(2,128)} %bitcast.2, ...), custom_call_target="tpu_custom_call" | custom-call | flops 14495514624 | bytes 12582912 | tf_op jit(solution)/shard_map/pallas_call | solution.py:860
  160.2 2.7 %shard_map.132 = (f32[2,64,6144]{2,1,0:T(8,128)}, f32[2,64,6144]{2,1,0:T(8,128)}) custom-call(f32[2,64,6144]{2,1,0:T(8,128)S(1)} %get-tuple-element.8.aligned_in, f32[2,64,4096]{2,1,0:T(8,128)S(1)} %get-tuple-element.9.done, f32[2,16,64,128]{3,2,1,0:T(8,128)S(1)} %get-tuple-element.10.bins, f32[1,64,2048]{2,1,0:T(8,128)S(1)} %get-tuple-element.11.ready, ...), custom_call_target="tpu_custom_call" | custom-call | tf_op jit(solution)/shard_map/pallas_call | solution.py:907

commit v5 on v4

--- a/solution.py
+++ b/solution.py
@@ -564,11 +564,11 @@
     def to_all_last(start):
         quad, place = lax.div(me, QUAD), lax.rem(me, QUAD)
         across = 2 * (1 - lax.div(quad, 2))
-        for target in (across, across + 1, quad + 1 - 2 * lax.rem(quad, 2)):
+        for target in (quad + 1 - 2 * lax.rem(quad, 2), quad, across, across + 1):
             for turn in range(QUAD):
+                if target is quad and turn == 0:
+                    continue
                 start(target * QUAD + lax.rem(place + turn, QUAD))
-        for turn in range(1, QUAD):
-            start(quad * QUAD + lax.rem(place + turn, QUAD))
 
     column = lax.broadcasted_iota(jnp.int32, (1, TF2), 1)
     total = height + 2 * MAXS

time: 164 us -> 164 us (level)
  no operation moved by 1% of the time
where the time goes in v5:
time: 164 us; the launch traced here: 163 us
  Pallas kernels  162 us (99%)
    pallas_call x1, Pallas kernels, kernel_whole(): pl.pallas_call(whole_kernel, out_shape=held, in_specs=[far] * len(large),...  160 us

profile of v5, /device:TPU:15, one launch (start us, length us, event | category | flops | bytes accessed | tf_op | source)
XLA Modules:
  0.0 163.0 jit_solution(6928729330205158759)
XLA Ops:
  0.6 159.6 %shard_map.131 = (f32[2,64,6144]{2,1,0:T(8,128)S(1)}, f32[2,64,4096]{2,1,0:T(8,128)S(1)}, f32[2,16,64,128]{3,2,1,0:T(8,128)S(1)}, f32[1,64,2048]{2,1,0:T(8,128)S...) custom-call(s32[2,12]{1,0:T(2,128)} %bitcast.3, s32[2,2,12]{2,1,0:T(2,128)} %bitcast.2, ...), custom_call_target="tpu_custom_call" | custom-call | flops 14495514624 | bytes 12582912 | tf_op jit(solution)/shard_map/pallas_call | solution.py:860
  160.3 2.7 %shard_map.132 = (f32[2,64,6144]{2,1,0:T(8,128)}, f32[2,64,6144]{2,1,0:T(8,128)}) custom-call(f32[2,64,6144]{2,1,0:T(8,128)S(1)} %get-tuple-element.8.aligned_in, f32[2,64,4096]{2,1,0:T(8,128)S(1)} %get-tuple-element.9.done, f32[2,16,64,128]{3,2,1,0:T(8,128)S(1)} %get-tuple-element.10.bins, f32[1,64,2048]{2,1,0:T(8,128)S(1)} %get-tuple-element.11.ready, ...), custom_call_target="tpu_custom_call" | custom-call | tf_op jit(solution)/shard_map/pallas_call | solution.py:907
